TPU v7x, 256 devices: a whole 4x4x8 slice. The times are simulated.
256 devices in a mesh: occ: 8 (over x, y_lo), vir: 8 (over z), con: 4 (over y_hi, core).
Axes of the slice: x: 4, y: 4 (y_hi: 2, y_lo: 2; y = y_hi * 2 + y_lo), z: 8, core: 2. Of those that a mesh axis runs over, the one named last changes fastest.
Arguments:
- amplitudes: bfloat16 [4096, 65536], P('occ', ('vir', 'con')), may hold values from -6 to 6
- integrals: bfloat16 [1024, 65536], P('occ', ('vir', 'con')), may hold values from -0.046875 to 0.046875
- occ_irrep: int32 [64], replicated, may hold values from 0 to 7
- ab_irrep: int32 [8], replicated, may hold values from 0 to 7
- cd_irrep: int32 [512], P(('vir', 'con')), may hold values from 0 to 7
Outputs:
- residual: bfloat16 [64, 64, 1024], P('occ', None, ('vir', 'con'))
All inputs are finite; a program needn't handle non-finite values.
Results may differ from a plain program's by a relative error of at most 0.0015.
Values may be sent and summed in bfloat16 or wider, within the bound.
No kernel may reach another device: no remote copies, remote signals or barrier semaphores. Data moves between devices by JAX's collectives and lax.ppermute only.
A program may use at most 64 MiB of HBM per device.

v0:
```python
import jax
import jax.numpy as jnp
from jax import lax
from jax.sharding import PartitionSpec as P

TILE = 128


def mask_columns(values, row_labels, col_labels):
    return jnp.where(
        row_labels[:, None] == col_labels[None, :], values, jnp.zeros((), values.dtype)
    )


def contract(operand, masked):
    return lax.dot_general(
        operand, masked, (((1,), (1,)), ((), ())), preferred_element_type=jnp.float32
    )


def per_device(amplitudes, integrals, occ_irrep, ab_irrep, cd_irrep):
    row_count, col_count = amplitudes.shape
    orbitals = occ_irrep.shape[0]
    local_count = orbitals // lax.axis_size("occ")
    first_orbital = lax.axis_index("occ") * local_count
    local_labels = lax.dynamic_slice_in_dim(occ_irrep, first_orbital, local_count)
    pair_labels = jnp.bitwise_xor(local_labels[:, None], occ_irrep[None, :]).reshape(row_count)
    col_labels = jnp.repeat(cd_irrep, TILE)
    ab_labels = jnp.repeat(ab_irrep, TILE)
    own_masked = mask_columns(amplitudes, pair_labels, col_labels)
    swapped = lax.all_to_all(
        amplitudes.reshape(local_count, orbitals, col_count),
        "occ",
        split_axis=1,
        concat_axis=0,
        tiled=True,
    )
    mirrored = jnp.transpose(swapped, (1, 0, 2)).reshape(row_count, col_count)
    mirrored = mask_columns(mirrored, pair_labels, col_labels)
    masked = mask_columns(
        lax.all_gather(integrals, "occ", axis=0, tiled=True), ab_labels, col_labels
    )
    partial_value = 2.0 * contract(own_masked, masked) - contract(mirrored, masked)
    slab_width = partial_value.shape[1]
    summed = lax.psum_scatter(
        partial_value.reshape(local_count, orbitals, slab_width),
        ("vir", "con"),
        scatter_dimension=2,
        tiled=True,
    )
    return summed.astype(jnp.bfloat16)


def solution(mesh):
    return jax.shard_map(
        per_device,
        mesh=mesh,
        in_specs=(P("occ", ("vir", "con")), P("occ", ("vir", "con")), P(), P(), P(("vir", "con"))),
        out_specs=P("occ", None, ("vir", "con")),
        check_vma=False,
    )
```

profile of v0, /device:TPU:8, one launch (start us, length us, event | category | flops | bytes accessed | tf_op | source)
XLA Modules:
  0.0 269.8 jit_solution(9335783254699288196)
XLA Ops:
  6.5 0.0 copy-start
  6.5 0.0 all-gather.2.cloned.1.call-start
  6.5 0.7 all-gather.2.cloned.1.call-update
  7.3 4.1 %copy.11 = bf16[8,64,2048]{2,0,1:T(8,128)(2,1)} copy(bf16[8,64,2048]{2,1,0:T(8,128)(2,1)} %bitcast.16) | data formatting | bytes 4194304 | tf_op jit(solution)/shard_map/reshape | solution.py:32
  11.3 5.9 %all-to-all-start = ((bf16[8,64,2048]{2,0,1:T(8,128)(2,1)}), bf16[8,64,2048]{2,0,1:T(8,128)(2,1)S(1)}, u32[]{:S(2)}, u32[]{:S(2)}) async-start(bf16[8,64,2048]{2,0,1:T(8,128)(2,1)} %copy.11), calls=%async_computation | async-start | bytes 4194304 | tf_op jit(solution)/shard_map/all_to_all | solution.py:31
  17.2 0.0 reduce-scatter.2.cloned.1.call-start
  17.2 0.1 dynamic_slice.3
  17.3 0.1 broadcast_xor_fusion
  17.4 0.1 xor.23
  17.5 0.1 broadcast_bitcast_fusion.1
  17.5 0.1 broadcast_bitcast_fusion
  17.6 36.5 %all-to-all-done = bf16[8,64,2048]{2,0,1:T(8,128)(2,1)S(1)} async-done(((bf16[8,64,2048]{2,0,1:T(8,128)(2,1)}), bf16[8,64,2048]{2,0,1:T(8,128)(2,1)S(1)}, u32[]{:S(2)}, u32[]{:S(2)}) %all-to-all-start) | async-done | bytes 2097184 | tf_op jit(solution)/shard_map/all_to_all | solution.py:31
  54.1 1.2 copy.13
  55.3 0.0 copy-start.1
  55.3 2.5 copy.14
  57.8 61.8 %all-gather.2.cloned.1.call-done = bf16[1024,2048]{1,0:T(8,128)(2,1)} async-done(((bf16[128,2048]{1,0:T(8,128)(2,1)}), bf16[1024,2048]{1,0:T(8,128)(2,1)}) %all-gather.2.cloned.1.call-update) | async-done | bytes 4194320 | tf_op jit(solution)/shard_map/all_gather | solution.py:41
  119.6 4.9 %fusion = f32[512,1024]{1,0:T(8,128)S(1)} fusion(bf16[512,2048]{1,0:T(8,128)(2,1)S(1)} %copy-done.1, s32[2048]{0:T(1024)S(1)} %broadcast_bitcast_fusion, s32[512]{0:T(512)S(1)} %xor.23, bf16[1024,2048]{1,0:T(8,128)(2,1)} %all-gather.2.cloned.1.call-done, s32[1024]{0:T(1024)S(1)} %broadcast_bitcast_fusion.1), kind=kOutput, calls=%fused_computation.3 | convolution fusion | flops 2153775104 | bytes 8402944 | tf_op jit(solution)/shard_map/dot_general | solution.py:16
  124.5 0.0 copy-done.2
  124.5 0.0 copy-done.5
  124.5 2.5 multiply_subtract_fusion
  127.0 2.7 %copy.15 = f32[8,64,1024]{1,2,0:T(8,128)} copy(f32[8,64,1024]{2,1,0:T(8,128)S(1)} %bitcast.15) | data formatting | bytes 4194304 | tf_op jit(solution)/shard_map/reshape | solution.py:46
  129.8 0.0 reduce-scatter.2.cloned.1.call-update
  129.8 131.7 %reduce-scatter.2.cloned.1.call-done = f32[8,64,32]{1,2,0:T(8,128)} async-done(((f32[8,64,1024]{1,2,0:T(8,128)}), f32[8,64,32]{1,2,0:T(8,128)}) %reduce-scatter.2.cloned.1.call-update) | async-done | bytes 65552 | tf_op jit(solution)/shard_map/reduce_scatter | solution.py:45
  261.4 1.5 convert_element_type.3
  (8 shorter events, 0.0 us)
Async XLA Ops:
  6.5 11.0 %copy-start = (s32[16]{0:T(128)S(1)}, s32[16]{0:T(128)}, u32[]{:S(2)}) copy-start(s32[16]{0:T(128)} %param.9) | copy-start | bytes 196
  6.5 113.0 %all-gather.2.cloned.1.call-start = ((), (), s32[]{:S(2)}) async-start(), calls=%async_computation.2 | async-start | bytes 4718592 | tf_op jit(solution)/shard_map/all_gather | solution.py:41
  11.3 5.9 %copy-start.3 = (s32[64]{0:T(128)S(1)}, s32[64]{0:T(128)}, u32[]{:S(2)}) copy-start(s32[64]{0:T(128)} %param.7) | copy-start | bytes 772
  11.3 6.1 %copy-start.4 = (s32[8]{0:T(128)S(1)}, s32[8]{0:T(128)}, u32[]{:S(2)}) copy-start(s32[8]{0:T(128)} %param.8) | copy-start | bytes 100
  11.3 42.8 %all-to-all-start = ((bf16[8,64,2048]{2,0,1:T(8,128)(2,1)}), bf16[8,64,2048]{2,0,1:T(8,128)(2,1)S(1)}, u32[]{:S(2)}, u32[]{:S(2)}) async-start(bf16[8,64,2048]{2,0,1:T(8,128)(2,1)} %copy.11), calls=%async_computation | async-start | bytes 4194304 | tf_op jit(solution)/shard_map/all_to_all | solution.py:31
  17.2 244.2 %reduce-scatter.2.cloned.1.call-start = ((), (), s32[]{:S(2)}) async-start(), calls=%async_computation.3 | async-start | bytes 4325376 | tf_op jit(solution)/shard_map/reduce_scatter | solution.py:45
  55.3 64.3 %copy-start.1 = (bf16[512,2048]{1,0:T(8,128)(2,1)S(1)}, bf16[512,2048]{1,0:T(8,128)(2,1)}, u32[]{:S(2)}) copy-start(bf16[512,2048]{1,0:T(8,128)(2,1)} %param.5) | copy-start | bytes 6291460
  119.6 4.9 %copy-start.2 = (bf16[8,64,2048]{2,1,0:T(8,128)(2,1)S(1)}, bf16[8,64,2048]{2,1,0:T(8,128)(2,1)}, u32[]{:S(2)}) copy-start(bf16[8,64,2048]{2,1,0:T(8,128)(2,1)} %copy.14) | copy-start | bytes 6291460
  119.6 4.9 %copy-start.5 = (bf16[1024,2048]{1,0:T(8,128)(2,1)S(1)}, bf16[1024,2048]{1,0:T(8,128)(2,1)}, u32[]{:S(2)}) copy-start(bf16[1024,2048]{1,0:T(8,128)(2,1)} %all-gather.2.cloned.1.call-done) | copy-start | bytes 12582916
Sparse Core Ops, SparseCore 0:
  9.1 110.3 all-gather.1
  129.9 131.5 reduce-scatter.1
where the time goes:
time: 271 us; the launch traced here: 270 us
  waiting for transfers between devices  231 us (85%)
  between operations  13.4 us (5%)
  local copies, waits for them, and re-layouts  10.8 us (4%)
  matrix products  7.4 us (3%)
  starting transfers between devices  5.89 us (2%)
    reduce_scatter x1, waiting for transfers between devices, per_device(): lax.psum_scatter(partial_value.reshape(local_count, orbitals, slab_width)...  132 us
    all_gather x1, waiting for transfers between devices, per_device(): lax.all_gather(integrals, 'occ', axis=0, tiled=True)  61.8 us
    all_to_all x1, waiting for transfers between devices, per_device(): lax.all_to_all(amplitudes.reshape(local_count, orbitals, col_count), 'occ...  36.5 us
    dot_general x2, matrix products, contract(): lax.dot_general(operand, masked, (((1,), (1,)), ((), ())), preferred_elem...  7.4 us
    all_to_all x1, starting transfers between devices, per_device(): lax.all_to_all(amplitudes.reshape(local_count, orbitals, col_count), 'occ...  5.89 us
  transfers between devices with their start and end apart: 3, of which 3 were waited for; matrix products, arithmetic and copies ran while one was open for 3% of the time, Pallas kernels for 0%

commit v1 on v0

v1 whole, which is shorter than its diff:
```python
import jax
import jax.numpy as jnp
from jax import lax
from jax.sharding import Mesh, PartitionSpec as P

TILE = 128


def shifted(axis, size, step):
    return lambda a: lax.ppermute(a, axis, [(i, (i + step) % size) for i in range(size)])


def per_device(amplitudes, integrals, occ_irrep, ab_irrep, cd_irrep):
    rows, cols = amplitudes.shape
    orbitals = occ_irrep.shape[0]
    nx, ny = lax.axis_size("x"), lax.axis_size("yl")
    groups = nx * ny
    local = orbitals // groups
    x, y = lax.axis_index("x"), lax.axis_index("yl")
    me = x * ny + y

    partner = shifted("yl", ny, 1)(integrals)
    blocks = [integrals, partner]
    owners = [me, x * ny + (1 - y)]
    for step in range(1, nx):
        move = shifted("x", nx, step)
        for block, other in ((integrals, y), (partner, 1 - y)):
            blocks.append(move(block))
            owners.append(((x - step) % nx) * ny + other)
    owners = jnp.stack(owners)

    mine = lax.dynamic_slice_in_dim(occ_irrep, me * local, local)
    pair = jnp.bitwise_xor(mine[:, None], occ_irrep[None, :]).reshape(rows)
    col = jnp.repeat(cd_irrep, TILE)
    masked_t = jnp.where(pair[:, None] == col[None, :], amplitudes, 0)
    masked_v = [
        jnp.where(ab_irrep[o] == col[None, :], b, 0) for o, b in zip(owners, blocks)
    ]
    slot = jnp.zeros((groups,), jnp.int32).at[owners].set(jnp.arange(groups, dtype=jnp.int32))
    part = lax.dot_general(
        jnp.concatenate(masked_v), masked_t, (((1,), (1,)), ((), ())),
        preferred_element_type=jnp.float32,
    )
    part = part.reshape(groups, 2, 2, TILE // 4, rows)
    part = jnp.take(part, slot, axis=0)

    core = lax.axis_index("core")
    keep = lax.dynamic_index_in_dim(part, core, 2, keepdims=False)
    send = lax.dynamic_index_in_dim(part, 1 - core, 2, keepdims=False)
    part = keep + shifted("core", 2, 1)(send)
    part = part.reshape(groups * 2, TILE // 4, rows)
    part = lax.all_to_all(part, ("vir", "yh"), 0, 0, tiled=True).sum(0)

    own = part.reshape(TILE // 4, local, groups, local).transpose(2, 0, 1, 3)
    got = lax.all_to_all(own, ("x", "yl"), 0, 0, tiled=True)
    own = own.transpose(2, 0, 3, 1)
    got = got.transpose(3, 0, 2, 1)
    out = 2.0 * own - got
    return out.reshape(local, orbitals, TILE // 4).astype(jnp.bfloat16)


def solution(mesh):
    occ, vir, con = (mesh.shape[a] for a in ("occ", "vir", "con"))
    split = Mesh(
        mesh.devices.reshape(occ // 2, 2, vir, 2, con // 2), ("x", "yl", "vir", "yh", "core")
    )
    cd = ("vir", "yh", "core")
    return jax.shard_map(
        per_device,
        mesh=split,
        in_specs=(P(("x", "yl"), cd), P(("x", "yl"), cd), P(), P(), P(cd)),
        out_specs=P(("x", "yl"), None, cd),
        check_vma=False,
    )
```

time: 271 us -> 119 us (0.44)
  waiting for transfers between devices: 231 us -> 25.9 us
  blocking collectives: 0 us -> 50.4 us
  other arithmetic: 1.62 us -> 19 us
  between operations: 13.4 us -> 0.12 us
  starting transfers between devices: 5.89 us -> 11.1 us
  local copies, waits for them, and re-layouts: 10.8 us -> 7.65 us
  matrix products: 7.4 us -> 4.63 us
    reduce_scatter x1 -> x0, waiting for transfers between devices: 132 us -> none  [per_device(): lax.psum_scatter(partial_value.reshape(local_count, orbitals, slab_width)...]
    all_gather x1 -> x0, waiting for transfers between devices: 61.8 us -> none  [per_device(): lax.all_gather(integrals, 'occ', axis=0, tiled=True)]
    all_to_all x0 -> x2, blocking collectives: none -> 50.4 us  [the longest x1 41.1 us: per_device(): part = lax.all_to_all(part, ('vir', 'yh'), 0, 0, tiled=True).sum(0)]
    all_to_all x1 -> x0, waiting for transfers between devices: 36.5 us -> none  [per_device(): lax.all_to_all(amplitudes.reshape(local_count, orbitals, col_count), 'occ...]
    ppermute x0 -> x8, waiting for transfers between devices: none -> 25.9 us  [shifted(): lax.ppermute(a, axis, [(i, (i + step) % size) for i in range(size)])]
    ppermute x0 -> x8, starting transfers between devices: none -> 11.1 us  [shifted(): lax.ppermute(a, axis, [(i, (i + step) % size) for i in range(size)])]
    unnamed x0 -> x7, other arithmetic: none -> 7.36 us
    reshape x2 -> x0, local copies, waits for them, and re-layouts: 6.8 us -> none  [the longest x1 4.07 us: per_device(): amplitudes.reshape(local_count, orbitals, col_count)]
  transfers between devices with their start and end apart: 3 -> 8, of which waited for: 3 -> 3; matrix products, arithmetic and copies ran while one was open for 3% -> 15% of each run, Pallas kernels for 0% -> 0%
where the time goes in v1:
time: 119 us
  blocking collectives  50.4 us (42%)
  waiting for transfers between devices  25.9 us (22%)
  other arithmetic  19 us (16%)
  starting transfers between devices  11.1 us (9%)
  local copies, waits for them, and re-layouts  7.65 us (6%)
  matrix products  4.63 us (4%)
    all_to_all x1, blocking collectives, per_device(): part = lax.all_to_all(part, ('vir', 'yh'), 0, 0, tiled=True).sum(0)  41.1 us
    ppermute x8, waiting for transfers between devices, shifted(): lax.ppermute(a, axis, [(i, (i + step) % size) for i in range(size)])  25.9 us
    ppermute x8, starting transfers between devices, shifted(): lax.ppermute(a, axis, [(i, (i + step) % size) for i in range(size)])  11.1 us
    all_to_all x1, blocking collectives, per_device(): got = lax.all_to_all(own, ('x', 'yl'), 0, 0, tiled=True)  9.33 us
    unnamed x7, other arithmetic  7.36 us
    eq x1, other arithmetic, per_device(): ab_irrep[o] == col[None, :]  5.71 us
    dot_general x1, matrix products, per_device(): lax.dot_general(jnp.concatenate(masked_v), masked_t, (((1,), (1,)), ((),...  4.63 us
  transfers between devices with their start and end apart: 8, of which 3 were waited for; matrix products, arithmetic and copies ran while one was open for 15% of the time, Pallas kernels for 0%

profile of v1, /device:TPU:8, one launch (start us, length us, event | category | flops | bytes accessed | tf_op | source)
XLA Modules:
  0.0 118.8 jit_solution(7991433189786934227)
XLA Ops:
  0.0 2.2 %collective-permute-start = (bf16[128,2048]{1,0:T(8,128)(2,1)}, bf16[128,2048]{1,0:T(8,128)(2,1)S(1)}, u32[]{:S(2)}, u32[]{:S(2)}) collective-permute-start(bf16[128,2048]{1,0:T(8,128)(2,1)} %param.6), channel_id=1, source_target_pairs={{0,32},{32,0},{1,33},{33,1},{2,34},{34,2},{3,35},{35,3},{4,36},{36... | collective-permute-start | bytes 1572872 | tf_op jit(solution)/shard_map/ppermute | solution.py:10
  2.2 2.5 %collective-permute-start.3 = (bf16[128,2048]{1,0:T(8,128)(2,1)}, bf16[128,2048]{1,0:T(8,128)(2,1)S(1)}, u32[]{:S(2)}, u32[]{:S(2)}) collective-permute-start(bf16[128,2048]{1,0:T(8,128)(2,1)} %param.6), channel_id=1, source_target_pairs={{0,128},{64,192},{128,0},{192,64},{1,129},{65,193},{129,1},{193,65... | collective-permute-start | bytes 1572872 | tf_op jit(solution)/shard_map/ppermute | solution.py:10
  4.7 1.4 %collective-permute-start.5 = (bf16[128,2048]{1,0:T(8,128)(2,1)}, bf16[128,2048]{1,0:T(8,128)(2,1)S(1)}, u32[]{:S(2)}, u32[]{:S(2)}) collective-permute-start(bf16[128,2048]{1,0:T(8,128)(2,1)} %param.6), channel_id=1, source_target_pairs={{0,192},{64,0},{128,64},{192,128},{1,193},{65,1},{129,65},{193,129... | collective-permute-start | bytes 1572872 | tf_op jit(solution)/shard_map/ppermute | solution.py:10
  9.0 1.6 %fusion.10 = (s32[1]{0:T(128)}, s32[1]{0:T(128)}, s32[1]{0:T(128)}, s32[1]{0:T(128)}, s32[1]{0:T(128)}, /*index=5*/s32[1]{0:T(128)}, s32[1]{0:T(128)}, s32[1]{0:T(128)}) fusion(s32[8]{0:T(128)} %param.8, s32[]{:T(128)S(6)} %select_n.122, s32[]{:T(128)S(6)} %select_n.118, s32[]{:T(128)S(6)} %select_n.116, s32[]{:T(128)S(6)} %select_n.114, s32[]{:T(128)S(6)} %select_n.112, ...), kind=kLoop, calls=%fused_computation.39 | loop fusion | bytes 96 | tf_op jit(solution)/shard_map/dynamic_slice | solution.py:37
  10.7 5.7 %bitcast_compare_fusion = (pred[2048]{0:T(1024)(128)(4,1)S(1)}, pred[2048]{0:T(1024)(128)(4,1)S(1)}, pred[2048]{0:T(1024)(128)(4,1)S(1)}, pred[2048]{0:T(1024)(1...) fusion(s32[]{:T(128)} %bitcast.17, s32[16]{0:T(128)} %param.9, ...), kind=kLoop, calls=%fused_computation.21 | loop fusion | flops 16384 | bytes 16480 | tf_op jit(solution)/shard_map/eq | solution.py:37
  16.4 1.9 %select_dynamic-update-slice_fusion.7 = bf16[1024,2048]{1,0:T(8,128)(2,1)} fusion(bf16[128,2048]{1,0:T(8,128)(2,1)} %param.6, pred[2048]{0:T(1024)(128)(4,1)S(1)} %get-tuple-element.12), kind=kLoop, calls=%fused_computation.17 | loop fusion | flops 262143 | bytes 1050624
  19.0 1.8 %collective-permute-start.4 = (bf16[128,2048]{1,0:T(8,128)(2,1)S(1)}, bf16[128,2048]{1,0:T(8,128)(2,1)S(1)}, u32[]{:S(2)}, u32[]{:S(2)}) collective-permute-start(bf16[128,2048]{1,0:T(8,128)(2,1)S(1)} %collective-permute-done), channel_id=1, source_target_pairs={{0,128},{64,192},{128,0},{192,64},{1,129},{65,193},{129,1},{193,65... | collective-permute-start | bytes 1572872 | tf_op jit(solution)/shard_map/ppermute | solution.py:10
  20.8 0.9 select_dynamic-update-slice_fusion.6
  21.7 2.5 %collective-permute-start.6 = (bf16[128,2048]{1,0:T(8,128)(2,1)S(1)}, bf16[128,2048]{1,0:T(8,128)(2,1)S(1)}, u32[]{:S(2)}, u32[]{:S(2)}) collective-permute-start(bf16[128,2048]{1,0:T(8,128)(2,1)S(1)} %collective-permute-done), channel_id=1, source_target_pairs={{0,192},{64,0},{128,64},{192,128},{1,193},{65,1},{129,65},{193,129... | collective-permute-start | bytes 1572872 | tf_op jit(solution)/shard_map/ppermute | solution.py:10
  24.2 0.9 select_dynamic-update-slice_fusion.5
  25.1 15.0 %collective-permute-done.2 = bf16[128,2048]{1,0:T(8,128)(2,1)S(1)} collective-permute-done((bf16[128,2048]{1,0:T(8,128)(2,1)S(1)}, bf16[128,2048]{1,0:T(8,128)(2,1)S(1)}, u32[]{:S(2)}, u32[]{:S(2)}) %collective-permute-start.2) | collective-permute-done | bytes 524320 | tf_op jit(solution)/shard_map/ppermute | solution.py:10
  40.1 0.9 select_dynamic-update-slice_fusion.4
  41.0 0.9 select_dynamic-update-slice_fusion.3
  41.9 8.1 %collective-permute-done.4 = bf16[128,2048]{1,0:T(8,128)(2,1)S(1)} collective-permute-done((bf16[128,2048]{1,0:T(8,128)(2,1)S(1)}, bf16[128,2048]{1,0:T(8,128)(2,1)S(1)}, u32[]{:S(2)}, u32[]{:S(2)}) %collective-permute-start.4) | collective-permute-done | bytes 524320 | tf_op jit(solution)/shard_map/ppermute | solution.py:10
  50.0 0.9 select_dynamic-update-slice_fusion.2
  50.9 0.9 select_dynamic-update-slice_fusion.1
  51.8 0.9 select_dynamic-update-slice_fusion
  52.7 4.6 %fusion = f32[1024,512]{1,0:T(8,128)S(1)} fusion(bf16[1024,2048]{1,0:T(8,128)(2,1)} %select_dynamic-update-slice_fusion, bf16[512,2048]{1,0:T(8,128)(2,1)S(1)} %copy-done, s32[2048]{0:T(1024)S(1)} %broadcast_bitcast_fusion, s32[512]{0:T(512)S(1)} %xor.23), kind=kOutput, calls=%fused_computation.3 | convolution fusion | flops 2149580800 | bytes 8398848 | tf_op jit(solution)/shard_map/dot_general | solution.py:40
  57.3 2.0 %gather_fusion = f32[8,2,2,32,512]{4,3,2,1,0:T(8,128)} fusion(f32[8,2,2,32,512]{4,3,2,1,0:T(8,128)S(1)} %bitcast.57, s32[1024]{0:T(1024)S(1)} %pad_clamp_fusion), kind=kCustom, calls=%fused_computation | custom fusion | bytes 4194336 | tf_op jit(solution)/shard_map/jit(_take)/gather | solution.py:45
  59.4 1.9 %broadcast_select_fusion = f32[8,2,2,32,512]{4,3,2,1,0:T(8,128)S(1)} fusion(f32[8,2,2,32,512]{4,3,2,1,0:T(8,128)} %gather_fusion, pred[8]{0:T(512)(128)(4,1)S(1)} %compare_and_fusion), kind=kLoop, calls=%fused_computation.8 | loop fusion | flops 524288 | bytes 4194312 | tf_op jit(solution)/shard_map/jit(_take)/select_n | solution.py:45
  61.5 2.8 %collective-permute-done.7 = f32[8,2,32,512]{3,2,1,0:T(8,128)} collective-permute-done((f32[8,2,32,512]{3,2,1,0:T(8,128)S(1)}, f32[8,2,32,512]{3,2,1,0:T(8,128)}, u32[]{:S(2)}, u32[]{:S(2)}) %collective-permute-start.7) | collective-permute-done | bytes 1048608 | tf_op jit(solution)/shard_map/ppermute | solution.py:10
  64.3 1.4 %bitcast_add_fusion = f32[8,2,32,512]{3,2,1,0:T(8,128)S(1)} fusion(f32[8,2,32,512]{3,2,1,0:T(8,128)} %collective-permute-done.7, f32[8,2,2,32,512]{4,3,2,1,0:T(8,128)S(1)} %broadcast_select_fusion, s32[]{:T(128)S(6)} %select_n.127), kind=kLoop, calls=%fused_computation.6 | loop fusion | flops 262144 | bytes 3145732 | tf_op jit(solution)/shard_map/add | solution.py:50
  65.7 41.1 %all_to_all.10 = f32[16,32,512]{2,1,0:T(8,128)S(1)} all-to-all(f32[16,32,512]{2,1,0:T(8,128)S(1)} %bitcast.54), channel_id=1, replica_groups=mesh['x'=4,'yl'=2,'vir'=8,'yh'=2,'core'=2] {'vir','yh'}, dimensions={0} | all-to-all | bytes 2097152 | tf_op jit(solution)/shard_map/all_to_all | solution.py:52
  107.2 9.3 %all_to_all.11 = f32[8,1,2048]{2,1,0:T(1,128)S(1)} all-to-all(f32[8,1,2048]{2,1,0:T(1,128)S(1)} %reshape.424), channel_id=1, replica_groups=mesh['x'=4,'yl'=2,'vir'=8,'yh'=2,'core'=2] {'x','yl'}, dimensions={0} | all-to-all | bytes 131072 | tf_op jit(solution)/shard_map/all_to_all | solution.py:55
  (31 shorter events, 6.4 us)
Async XLA Ops:
  0.0 18.4 %collective-permute-start = (bf16[128,2048]{1,0:T(8,128)(2,1)}, bf16[128,2048]{1,0:T(8,128)(2,1)S(1)}, u32[]{:S(2)}, u32[]{:S(2)}) collective-permute-start(bf16[128,2048]{1,0:T(8,128)(2,1)} %param.6), channel_id=1, source_target_pairs={{0,32},{32,0},{1,33},{33,1},{2,34},{34,2},{3,35},{35,3},{4,36},{36... | collective-permute-start | bytes 1572872 | tf_op jit(solution)/shard_map/ppermute | solution.py:10
  2.2 19.5 %collective-permute-start.1 = (bf16[128,2048]{1,0:T(8,128)(2,1)}, bf16[128,2048]{1,0:T(8,128)(2,1)S(1)}, u32[]{:S(2)}, u32[]{:S(2)}) collective-permute-start(bf16[128,2048]{1,0:T(8,128)(2,1)} %param.6), channel_id=1, source_target_pairs={{0,64},{64,128},{128,192},{192,0},{1,65},{65,129},{129,193},{193,1... | collective-permute-start | bytes 1572872 | tf_op jit(solution)/shard_map/ppermute | solution.py:10
  2.2 38.8 %collective-permute-start.3 = (bf16[128,2048]{1,0:T(8,128)(2,1)}, bf16[128,2048]{1,0:T(8,128)(2,1)S(1)}, u32[]{:S(2)}, u32[]{:S(2)}) collective-permute-start(bf16[128,2048]{1,0:T(8,128)(2,1)} %param.6), channel_id=1, source_target_pairs={{0,128},{64,192},{128,0},{192,64},{1,129},{65,193},{129,1},{193,65... | collective-permute-start | bytes 1572872 | tf_op jit(solution)/shard_map/ppermute | solution.py:10
  4.7 46.2 %collective-permute-start.5 = (bf16[128,2048]{1,0:T(8,128)(2,1)}, bf16[128,2048]{1,0:T(8,128)(2,1)S(1)}, u32[]{:S(2)}, u32[]{:S(2)}) collective-permute-start(bf16[128,2048]{1,0:T(8,128)(2,1)} %param.6), channel_id=1, source_target_pairs={{0,192},{64,0},{128,64},{192,128},{1,193},{65,1},{129,65},{193,129... | collective-permute-start | bytes 1572872 | tf_op jit(solution)/shard_map/ppermute | solution.py:10
  18.4 34.3 %copy-start = (bf16[512,2048]{1,0:T(8,128)(2,1)S(1)}, bf16[512,2048]{1,0:T(8,128)(2,1)}, u32[]{:S(2)}) copy-start(bf16[512,2048]{1,0:T(8,128)(2,1)} %param.5) | copy-start | bytes 6291460
  18.4 21.7 %collective-permute-start.2 = (bf16[128,2048]{1,0:T(8,128)(2,1)S(1)}, bf16[128,2048]{1,0:T(8,128)(2,1)S(1)}, u32[]{:S(2)}, u32[]{:S(2)}) collective-permute-start(bf16[128,2048]{1,0:T(8,128)(2,1)S(1)} %collective-permute-done), channel_id=1, source_target_pairs={{0,64},{64,128},{128,192},{192,0},{1,65},{65,129},{129,193},{193,1... | collective-permute-start | bytes 1572872 | tf_op jit(solution)/shard_map/ppermute | solution.py:10
  19.0 31.0 %collective-permute-start.4 = (bf16[128,2048]{1,0:T(8,128)(2,1)S(1)}, bf16[128,2048]{1,0:T(8,128)(2,1)S(1)}, u32[]{:S(2)}, u32[]{:S(2)}) collective-permute-start(bf16[128,2048]{1,0:T(8,128)(2,1)S(1)} %collective-permute-done), channel_id=1, source_target_pairs={{0,128},{64,192},{128,0},{192,64},{1,129},{65,193},{129,1},{193,65... | collective-permute-start | bytes 1572872 | tf_op jit(solution)/shard_map/ppermute | solution.py:10
  21.7 30.1 %collective-permute-start.6 = (bf16[128,2048]{1,0:T(8,128)(2,1)S(1)}, bf16[128,2048]{1,0:T(8,128)(2,1)S(1)}, u32[]{:S(2)}, u32[]{:S(2)}) collective-permute-start(bf16[128,2048]{1,0:T(8,128)(2,1)S(1)} %collective-permute-done), channel_id=1, source_target_pairs={{0,192},{64,0},{128,64},{192,128},{1,193},{65,1},{129,65},{193,129... | collective-permute-start | bytes 1572872 | tf_op jit(solution)/shard_map/ppermute | solution.py:10
  61.4 2.9 %collective-permute-start.7 = (f32[8,2,32,512]{3,2,1,0:T(8,128)S(1)}, f32[8,2,32,512]{3,2,1,0:T(8,128)}, u32[]{:S(2)}, u32[]{:S(2)}) collective-permute-start(f32[8,2,32,512]{3,2,1,0:T(8,128)S(1)} %dynamic-slice_bitcast_fusion), channel_id=1, source_target_pairs={{0,1},{1,0},{2,3},{3,2},{4,5},{5,4},{6,7},{7,6},{8,9},{9,8},{10,11... | collective-permute-start | bytes 3145736 | tf_op jit(solution)/shard_map/ppermute | solution.py:10

commit v2 on v1

v2 whole, which is shorter than its diff:
```python
import functools

import jax
import jax.numpy as jnp
from jax import lax
from jax.experimental import pallas as pl
from jax.experimental.pallas import tpu as pltpu
from jax.sharding import Mesh, PartitionSpec as P

TILE = 128
ROWS = 256
SCALES = 8
STEP = 2.0**14
FIRST = 10
DIRECT = 6
MIB = 1 << 20
SMEM = pl.BlockSpec(memory_space=pltpu.SMEM)
VMEM = pl.BlockSpec(memory_space=pltpu.VMEM)
ANY = pl.BlockSpec(memory_space=pl.ANY)


def shifted(axis, size, step):
    return lambda a: lax.ppermute(a, axis, [(i, (i + step) % size) for i in range(size)])


def cost(us):
    return pl.CostEstimate(flops=int(us * 1.1e9), bytes_accessed=0, transcendentals=0)


def params(mib):
    return pltpu.CompilerParams(vmem_limit_bytes=mib * MIB)


def pack_kernel(skip, where, ab, cd, v, more, out, count):
    slots = out.shape[1] // TILE
    mine = ab[where[0]]
    for c in range(count.shape[0]):
        count[c] = 0

    @pl.loop(0, cd.shape[0])
    def _(t):
        label = cd[t]
        slot = count[label] - skip
        count[label] = count[label] + 1

        @pl.when((label == mine) & (slot >= 0) & (slot < slots))
        def _():
            out[:, pl.ds(pl.multiple_of(slot * TILE, TILE), TILE)] = v[
                :, pl.ds(pl.multiple_of(t * TILE, TILE), TILE)
            ]

    @pl.loop(jnp.clip(count[mine] - skip, 0, slots), slots)
    def _(slot):
        out[:, pl.ds(pl.multiple_of(slot * TILE, TILE), TILE)] = jnp.zeros((v.shape[0], TILE), v.dtype)

    most = count[ab[0]]
    for a in range(1, ab.shape[0]):
        most = jnp.maximum(most, count[ab[a]])
    more[0] = (most > skip + slots).astype(jnp.int32)


def pack(skip, slots, where, ab, cd, v):
    return pl.pallas_call(
        functools.partial(pack_kernel, skip),
        out_shape=[
            jax.ShapeDtypeStruct((1,), jnp.int32),
            jax.ShapeDtypeStruct((v.shape[0], slots * TILE), v.dtype),
        ],
        in_specs=[SMEM, SMEM, SMEM, VMEM],
        out_specs=[SMEM, VMEM],
        scratch_shapes=[pltpu.SMEM((8,), jnp.int32)],
        compiler_params=params(4),
        cost_estimate=cost(2.0),
        name="pack_integrals",
    )(where, ab, cd, v)


def one_hot(shape, spot):
    match = lax.broadcasted_iota(jnp.int32, shape, 0) == spot
    return match.astype(jnp.float32).astype(jnp.bfloat16)


def rank_kernel(where, occ, ab, occ_row, labels, rank, spots, over):
    orbitals, rows = occ_row.shape[1], labels.shape[1]
    local = rows // orbitals
    irreps, abt = 8, ab.shape[0]
    me, mine = where[0], ab[where[1]]
    for i in range(local):
        labels[:, i * orbitals : (i + 1) * orbitals] = occ_row[...] ^ occ[me * local + i]

    label = labels[...]
    is_label = lax.broadcasted_iota(jnp.int32, (irreps, rows), 0) == label
    marks = is_label.astype(jnp.float32).astype(jnp.bfloat16)

    @pl.loop(0, rows // TILE)
    def _(k):
        first = pl.multiple_of(k * TILE, TILE)
        shape = (rows, TILE)
        before = lax.broadcasted_iota(jnp.int32, shape, 0) < first + lax.broadcasted_iota(
            jnp.int32, shape, 1
        )
        ahead = jnp.dot(
            marks, before.astype(jnp.float32).astype(jnp.bfloat16), preferred_element_type=jnp.float32
        )
        own = lax.broadcasted_iota(jnp.int32, (irreps, TILE), 0) == labels[:, pl.ds(first, TILE)]
        rank[:, pl.ds(first, TILE)] = jnp.sum(
            jnp.where(own, ahead, 0.0), axis=0, keepdims=True
        ).astype(jnp.int32)

    column = lax.broadcasted_iota(jnp.int32, (abt, orbitals), 0)
    partner = occ_row[...]
    want = jnp.zeros((abt, orbitals), jnp.int32)
    for v in range(abt):
        want = jnp.where(column == v, ab[v], want)
    want = want ^ partner
    of_irrep = lax.broadcasted_iota(jnp.int32, (irreps, orbitals), 0) == partner
    count = jnp.sum(of_irrep.astype(jnp.float32), axis=1, keepdims=True)
    met = jnp.zeros((abt, orbitals), jnp.float32)
    for c in range(irreps):
        met = jnp.where(want == c, count[c : c + 1, :], met)
    shape = (orbitals, TILE)
    group = lax.broadcasted_iota(jnp.int32, shape, 0) // local == lax.broadcasted_iota(jnp.int32, shape, 1)
    held = jnp.dot(
        met.astype(jnp.bfloat16),
        group.astype(jnp.float32).astype(jnp.bfloat16),
        preferred_element_type=jnp.float32,
    )
    over[0] = (jnp.max(held) > ROWS - SCALES).astype(jnp.int32)

    which = lax.broadcasted_iota(jnp.int32, (8, rows), 0)
    place = rank[...]
    values = jnp.where(
        which == 0, label, jnp.where(which == 1, place % 256, jnp.where(which == 2, place // 256, 0))
    )
    values = values.astype(jnp.float32).astype(jnp.bfloat16)

    @pl.loop(0, spots.shape[1] // TILE)
    def _(owner):
        lane = lax.broadcasted_iota(jnp.int32, (1, TILE), 1)
        j, i = lane // local, lane % local
        source = jnp.where(j < local, i * orbitals + owner * local + j, -1)
        moved = jnp.dot(
            values, one_hot((rows, TILE), source), preferred_element_type=jnp.float32
        ).astype(jnp.int32)
        here = (moved[0:1] == mine) & (j < local)
        spots[:, pl.ds(pl.multiple_of(owner * TILE, TILE), TILE)] = jnp.where(
            here, moved[1:2] + 256 * moved[2:3], -1
        )


def ranks(where, occ, ab, rows, groups):
    return pl.pallas_call(
        rank_kernel,
        out_shape=[
            jax.ShapeDtypeStruct((1, rows), jnp.int32),
            jax.ShapeDtypeStruct((1, rows), jnp.int32),
            jax.ShapeDtypeStruct((1, groups * TILE), jnp.int32),
            jax.ShapeDtypeStruct((1,), jnp.int32),
        ],
        in_specs=[SMEM, SMEM, SMEM, VMEM],
        out_specs=[VMEM, VMEM, VMEM, SMEM],
        compiler_params=params(4),
        cost_estimate=cost(3.3),
        name="ranks",
    )(where, occ, ab, occ.reshape(1, -1))


def select_kernel(skip, after, ab, cd, labels, rank, t, *rest):
    out, hot, tile_of, count = rest[after:]
    tiles, slots = cd.shape[0], out.shape[1] // TILE
    for c in range(count.shape[0]):
        count[c] = 0

    @pl.loop(0, tiles)
    def _(i):
        label = cd[i]
        tile_of[label * tiles + count[label]] = i
        count[label] = count[label] + 1

    @pl.loop(0, ab.shape[0])
    def _(v):
        want = ab[v]

        @pl.when(first_of(ab, v) == v)
        def _():
            hot[...] = one_hot(hot.shape, jnp.where(labels[...] == want, rank[...], -1))
            used = jnp.clip(count[want] - skip, 0, slots)

            @pl.loop(0, used)
            def _(s):
                i = tile_of[want * tiles + skip + s]
                piece = t[:, pl.ds(pl.multiple_of(i * TILE, TILE), TILE)]
                rows_in = jnp.dot(hot[...], piece, preferred_element_type=jnp.float32)
                out[v, pl.ds(pl.multiple_of(s * TILE, TILE), TILE), :] = jnp.transpose(rows_in).astype(
                    jnp.bfloat16
                )

            @pl.loop(used, slots)
            def _(s):
                out[v, pl.ds(pl.multiple_of(s * TILE, TILE), TILE), :] = jnp.zeros(
                    (TILE, out.shape[2]), jnp.bfloat16
                )


def first_of(ab, v):
    want = ab[v]
    first = jnp.int32(0)
    for a in reversed(range(ab.shape[0])):
        first = jnp.where(ab[a] == want, a, first)
    return first


def select(skip, slots, ab, cd, labels, rank, t, after):
    return pl.pallas_call(
        functools.partial(select_kernel, skip, len(after)),
        out_shape=jax.ShapeDtypeStruct((ab.shape[0], slots * TILE, ROWS), t.dtype),
        in_specs=[SMEM, SMEM, VMEM, VMEM, VMEM] + [ANY] * len(after),
        out_specs=VMEM,
        scratch_shapes=[
            pltpu.VMEM((ROWS, t.shape[0]), jnp.bfloat16),
            pltpu.SMEM((8 * cd.shape[0],), jnp.int32),
            pltpu.SMEM((8,), jnp.int32),
        ],
        compiler_params=params(12),
        cost_estimate=cost(5.0),
        name="select_amplitudes",
    )(ab, cd, labels, rank, t, *after)


def product_kernel(sizes, where, owners, ab, t, *rest):
    pieces, (keep, send, largest, acc) = list(rest[:-4]), rest[-4:]
    core = where[2]
    part = acc.shape[0] // 4
    most = jnp.zeros((8, acc.shape[1]), jnp.float32)
    for b, size in enumerate(sizes):
        v = owners[b]
        f = first_of(ab, v)
        first = 0
        for k in range(size):
            piece = pieces.pop(0)
            last = first + piece.shape[1]
            x = jnp.dot(piece[...], t[f, first:last, :], preferred_element_type=jnp.float32)
            acc[...] = x if k == 0 else acc[...] + x
            first = last
        most = jnp.maximum(most, jnp.max(jnp.abs(acc[...]).reshape(-1, 8, acc.shape[1]), axis=0))
        for y in range(2):
            for out, c in ((keep, core), (send, 1 - core)):
                row = pl.multiple_of((2 * y + c) * part, part)
                out[v, y] = acc[pl.ds(row, part), :]
    largest[...] = jnp.full(largest.shape, jnp.max(most), jnp.float32)


def product(where, owners, ab, t, blocks):
    shape = jax.ShapeDtypeStruct((t.shape[0], 2, TILE // 4, t.shape[2]), jnp.float32)
    pieces = [piece for block in blocks for piece in block]
    return pl.pallas_call(
        functools.partial(product_kernel, [len(block) for block in blocks]),
        out_shape=[shape, shape, jax.ShapeDtypeStruct((8, TILE), jnp.float32)],
        in_specs=[SMEM] * 3 + [VMEM] * (1 + len(pieces)),
        out_specs=[VMEM, VMEM, VMEM],
        scratch_shapes=[pltpu.VMEM((TILE, t.shape[2]), jnp.float32)],
        compiler_params=params(12),
        cost_estimate=cost(2.5),
        name="product",
    )(where, owners, ab, t, *pieces)


def combine_kernel(keep, got, a, b, out):
    top = (a[...] + b[...])[0:1, :]
    up, down = jnp.ones_like(top), jnp.ones_like(top)
    for bits in (64, 32, 8, 4, 2, 1):
        fits = top * (up * 2.0**bits) <= 2.0**15
        up = jnp.where(fits, up * 2.0**bits, up)
        down = jnp.where(fits, down * 2.0**-bits, down)
    lane = lax.broadcasted_iota(jnp.int32, top.shape, 1)
    parts = jnp.zeros_like(top)
    for i in range(SCALES):
        parts = jnp.where(lane == TILE - SCALES + i, jnp.maximum(down, 1.0 / STEP), parts)
        down = jnp.where(down < 1.0 / STEP, down * STEP, 1.0)
    up = jnp.concatenate([up, jnp.where(lane < TILE - SCALES, up, 0.0)], axis=1)
    parts = jnp.concatenate([jnp.zeros_like(top), parts], axis=1)
    for v in range(keep.shape[0]):
        for y in range(keep.shape[1]):
            out[v * keep.shape[1] + y] = (keep[v, y] + got[v, y]) * up + parts


def combine(keep, got, a, b):
    return pl.pallas_call(
        combine_kernel,
        out_shape=jax.ShapeDtypeStruct((keep.shape[0] * keep.shape[1],) + keep.shape[2:], jnp.float32),
        in_specs=[VMEM] * 4,
        out_specs=VMEM,
        compiler_params=params(6),
        cost_estimate=cost(1.2),
        name="combine",
    )(keep, got, a, b)


def spread_kernel(where, ab, labels, rank, spots, parts, own, send):
    total = jnp.zeros(parts.shape[1:], jnp.float32)
    for z in range(parts.shape[0]):
        part = parts[z]
        down = part[0:1, ROWS - SCALES : ROWS - SCALES + 1]
        for i in range(1, SCALES):
            down *= part[0:1, ROWS - SCALES + i : ROWS - SCALES + i + 1]
        total += part * down
    high = total.astype(jnp.bfloat16)
    rest = total - high.astype(jnp.float32)
    middle = rest.astype(jnp.bfloat16)
    low = (rest - middle.astype(jnp.float32)).astype(jnp.bfloat16)
    split = jnp.concatenate([high, middle, low], axis=0)
    n = total.shape[0]

    def placed(spot):
        x = jnp.dot(split, one_hot((total.shape[1], spot.shape[1]), spot), preferred_element_type=jnp.float32)
        return x[:n] + (x[n : 2 * n] + x[2 * n :])

    for o in range(0, send.shape[0], 2):
        x = placed(spots[:, o * TILE : (o + 2) * TILE])
        send[o] = x[:, :TILE]
        send[o + 1] = x[:, TILE:]
    mine = ab[where[1]]
    for k in range(0, own.shape[1], 2 * TILE):
        span = slice(k, k + 2 * TILE)
        own[:, span] = placed(jnp.where(labels[:, span] == mine, rank[:, span], -1))


def spread(where, ab, labels, rank, spots, parts):
    return pl.pallas_call(
        spread_kernel,
        out_shape=[
            jax.ShapeDtypeStruct((parts.shape[1], labels.shape[1]), jnp.float32),
            jax.ShapeDtypeStruct((spots.shape[1] // TILE, parts.shape[1], TILE), jnp.float32),
        ],
        in_specs=[SMEM, SMEM] + [VMEM] * 4,
        out_specs=[VMEM, VMEM],
        compiler_params=params(6),
        cost_estimate=cost(1.7),
        name="spread",
    )(where, ab, labels, rank, spots, parts)


def finish_kernel(own, got, out, turned):
    local, orbitals, width = turned.shape
    for o in range(got.shape[0]):
        x = jnp.transpose(got[o])
        for i in range(local):
            turned[i, o * local : (o + 1) * local, :] = x[i * local : (i + 1) * local, :]
    for i in range(local):
        mine = own[:, i * orbitals : (i + 1) * orbitals]
        out[i * width : (i + 1) * width, :] = (2.0 * mine - jnp.transpose(turned[i])).astype(jnp.bfloat16)


def finish(own, got, local, orbitals):
    width = own.shape[0]
    return pl.pallas_call(
        finish_kernel,
        out_shape=jax.ShapeDtypeStruct((local * width, orbitals), jnp.bfloat16),
        in_specs=[VMEM, VMEM],
        out_specs=VMEM,
        scratch_shapes=[pltpu.VMEM((local, orbitals, width), jnp.float32)],
        compiler_params=params(4),
        cost_estimate=cost(0.4),
        name="finish",
    )(own, got)


def take_kernel(first, v, after, out):
    out[...] = v[:, first : first + out.shape[1]]


def take(v, first, last, after):
    return pl.pallas_call(
        functools.partial(take_kernel, first),
        out_shape=jax.ShapeDtypeStruct((v.shape[0], last - first), v.dtype),
        in_specs=[VMEM, ANY],
        out_specs=VMEM,
        compiler_params=params(4),
        name="take",
    )(v, after)


def gather(v, direct, after):
    nx, ny = lax.axis_size("x"), lax.axis_size("yl")
    swap = shifted("yl", ny, 1)
    moves = [shifted("x", nx, step) for step in range(1, nx)]
    partner = swap(v)
    own = [move(v) for move in moves]
    head = take(partner, 0, direct * TILE, after)
    blocks = [[v], [partner]]
    for move, block in zip(moves, own, strict=True):
        blocks += [[block], [move(head)]]
    tails = []
    if direct * TILE < v.shape[1]:
        for k, block in enumerate(own):
            tails.append(take(block, direct * TILE, v.shape[1], head))
            blocks[2 * k + 3].append(swap(tails[-1]))
    return blocks, tails


def owners_of():
    nx, ny = lax.axis_size("x"), lax.axis_size("yl")
    x, y = lax.axis_index("x"), lax.axis_index("yl")
    owners = []
    for step in range(nx):
        first = ((x - step) % nx) * ny
        owners += [first + y, first + 1 - y]
    return jnp.stack(owners).astype(jnp.int32)


def dense(amplitudes, integrals, occ_irrep, ab_irrep, cd_irrep):
    rows, cols = amplitudes.shape
    orbitals = occ_irrep.shape[0]
    groups = lax.axis_size("x") * lax.axis_size("yl")
    local = orbitals // groups
    me = lax.axis_index("x") * lax.axis_size("yl") + lax.axis_index("yl")
    blocks = lax.all_to_all(
        jnp.broadcast_to(integrals, (groups,) + integrals.shape), ("x", "yl"), 0, 0, tiled=True
    )
    mine = lax.dynamic_slice_in_dim(occ_irrep, me * local, local)
    pair = jnp.bitwise_xor(mine[:, None], occ_irrep[None, :]).reshape(rows)
    col = jnp.repeat(cd_irrep, TILE)
    masked_t = jnp.where(pair[:, None] == col[None, :], amplitudes, 0)
    masked_v = jnp.where(ab_irrep[:, None, None] == col[None, None, :], blocks, 0)
    part = lax.dot_general(
        masked_v.reshape(-1, cols), masked_t, (((1,), (1,)), ((), ())), preferred_element_type=jnp.float32
    )
    part = part.reshape(groups * 4, TILE // 4, rows)
    part = lax.all_to_all(part, ("vir", "yh", "core"), 0, 0, tiled=True).sum(0)
    own = part.reshape(TILE // 4, local, groups, local).transpose(2, 0, 1, 3)
    got = lax.all_to_all(own, ("x", "yl"), 0, 0, tiled=True)
    out = 2.0 * own.transpose(2, 0, 3, 1) - got.transpose(3, 0, 2, 1)
    return out.reshape(local, orbitals, TILE // 4).astype(jnp.bfloat16)


def per_device(amplitudes, integrals, occ_irrep, ab_irrep, cd_irrep):
    groups = lax.axis_size("x") * lax.axis_size("yl")
    orbitals = occ_irrep.shape[0]
    rows = amplitudes.shape[0]
    me = lax.axis_index("x") * lax.axis_size("yl") + lax.axis_index("yl")
    where = jnp.stack([me, lax.axis_index("vir"), lax.axis_index("core")]).astype(jnp.int32)
    owners = owners_of()
    tiles = cd_irrep.shape[0]

    def partial_sums(skip, slots, direct, found, packed):
        blocks, tails = gather(packed, direct, found[1])
        selected = select(skip, slots, ab_irrep, cd_irrep, *found[:2], amplitudes, tails)
        return product(where, owners, ab_irrep, selected, blocks)

    more, packed = pack(0, FIRST, where, ab_irrep, cd_irrep, integrals)
    found = ranks(where, occ_irrep, ab_irrep, rows, groups)
    sums = partial_sums(0, FIRST, DIRECT, found, packed)

    def rest(sums, v, found):
        _, packed = pack(FIRST, tiles - FIRST, where, ab_irrep, cd_irrep, v)
        added = partial_sums(FIRST, tiles - FIRST, tiles - FIRST, found, packed)
        return jax.tree.map(jnp.add, list(sums), list(added))

    keep, send, largest = lax.cond(
        more[0] > 0, rest, lambda sums, v, found: list(sums), list(sums), integrals, found
    )
    labels, rank, spots, over = found
    other = shifted("core", 2, 1)
    part = combine(keep, other(send), largest, other(largest)).astype(jnp.float16)
    part = lax.all_to_all(part, ("vir", "yh"), 0, 0, tiled=True).astype(jnp.float32)
    own, send = spread(where, ab_irrep, labels, rank, spots, part)
    got = lax.all_to_all(send, ("x", "yl"), 0, 0, tiled=True)
    out = lax.cond(
        over[0] > 0,
        lambda own, got, *a: jnp.swapaxes(dense(*a), 1, 2).reshape(-1, orbitals),
        lambda own, got, *a: finish(own, got, rows // orbitals, orbitals),
        *(own, got, amplitudes, integrals, occ_irrep, ab_irrep, cd_irrep),
    )
    return jnp.swapaxes(out.reshape(rows // orbitals, -1, orbitals), 1, 2)


def solution(mesh):
    occ, vir, con = (mesh.shape[a] for a in ("occ", "vir", "con"))
    split = Mesh(
        mesh.devices.reshape(occ // 2, 2, vir, 2, con // 2), ("x", "yl", "vir", "yh", "core")
    )
    cd = ("vir", "yh", "core")
    return jax.shard_map(
        per_device,
        mesh=split,
        in_specs=(P(("x", "yl"), cd), P(("x", "yl"), cd), P(), P(), P(cd)),
        out_specs=P(("x", "yl"), None, cd),
        check_vma=False,
    )
```

time: 119 us -> 74.6 us (0.63)
  blocking collectives: 50.4 us -> 24.2 us
  other arithmetic: 19 us -> 0.15 us
  Pallas kernels: 0 us -> 15.6 us
  waiting for transfers between devices: 25.9 us -> 11.6 us
  starting transfers between devices: 11.1 us -> 20 us
  local copies, waits for them, and re-layouts: 7.65 us -> 1.38 us
  matrix products: 4.63 us -> 0 us
  between operations: 0.12 us -> 1.63 us
    all_to_all x2 -> x1, blocking collectives: 50.4 us -> 24.2 us  [per_device(): lax.all_to_all(part, ('vir', 'yh'), 0, 0, tiled=True).astype(jnp.float32)]
    ppermute x8 -> x12, waiting for transfers between devices: 25.9 us -> 6.87 us  [shifted(): lax.ppermute(a, axis, [(i, (i + step) % size) for i in range(size)])]
    pallas_call x0 -> x11, Pallas kernels: none -> 15.6 us  [the longest x1 6.69 us: select(): pl.pallas_call(functools.partial(select_kernel, skip, len(after)), out_sh...]
    unnamed x7 -> x0, other arithmetic: 7.36 us -> none
    all_to_all x0 -> x1, starting transfers between devices: none -> 6.54 us  [per_device(): got = lax.all_to_all(send, ('x', 'yl'), 0, 0, tiled=True)]
    eq x1 -> x0, other arithmetic: 5.71 us -> none  [per_device(): ab_irrep[o] == col[None, :]]
    all_to_all x0 -> x1, waiting for transfers between devices: none -> 4.74 us  [per_device(): got = lax.all_to_all(send, ('x', 'yl'), 0, 0, tiled=True)]
    dot_general x1 -> x0, matrix products: 4.63 us -> none  [per_device(): lax.dot_general(jnp.concatenate(masked_v), masked_t, (((1,), (1,)), ((),...]
  transfers between devices with their start and end apart: 8 -> 13, of which waited for: 3 -> 6; matrix products, arithmetic and copies ran while one was open for 15% -> 1% of each run, Pallas kernels for 0% -> 13%
where the time goes in v2:
time: 74.6 us; the launch traced here: 74.7 us
  blocking collectives  24.2 us (32%)
  starting transfers between devices  20 us (27%)
  Pallas kernels  15.6 us (21%)
  waiting for transfers between devices  11.6 us (16%)
  between operations  1.63 us (2%)
  local copies, waits for them, and re-layouts  1.38 us (2%)
    all_to_all x1, blocking collectives, per_device(): lax.all_to_all(part, ('vir', 'yh'), 0, 0, tiled=True).astype(jnp.float32)  24.2 us
    ppermute x12, starting transfers between devices, shifted(): lax.ppermute(a, axis, [(i, (i + step) % size) for i in range(size)])  13.4 us
    ppermute x12, waiting for transfers between devices, shifted(): lax.ppermute(a, axis, [(i, (i + step) % size) for i in range(size)])  6.87 us
    pallas_call x1, Pallas kernels, select(): pl.pallas_call(functools.partial(select_kernel, skip, len(after)), out_sh...  6.69 us
    all_to_all x1, starting transfers between devices, per_device(): got = lax.all_to_all(send, ('x', 'yl'), 0, 0, tiled=True)  6.54 us
    all_to_all x1, waiting for transfers between devices, per_device(): got = lax.all_to_all(send, ('x', 'yl'), 0, 0, tiled=True)  4.74 us
    pallas_call x1, Pallas kernels, ranks(): pl.pallas_call(rank_kernel, out_shape=[jax.ShapeDtypeStruct((1, rows), jn...  3.09 us
    pallas_call x1, Pallas kernels, pack(): pl.pallas_call(functools.partial(pack_kernel, skip), out_shape=[jax.Shape...  1.98 us
  transfers between devices with their start and end apart: 13, of which 6 were waited for; matrix products, arithmetic and copies ran while one was open for 1% of the time, Pallas kernels for 13%

profile of v2, /device:TPU:8, one launch (start us, length us, event | category | flops | bytes accessed | tf_op | source)
XLA Modules:
  0.0 74.7 jit_solution(8341621588821015278)
XLA Ops:
  0.1 2.0 %pack_integrals.3 = (s32[1]{0:T(128)}, bf16[128,1280]{1,0:T(8,128)(2,1)S(1)}) custom-call(s32[3]{0:T(128)S(1)} %pad_add_fusion.where, s32[8]{0:T(128)} %ab.9, s32[16]{0:T(128)} %cd.3, bf16[128,2048]{1,0:T(8,128)(2,1)} %v.1), custom_call_target="tpu_custom_call" | custom-call | flops 2200000000 | tf_op jit(solution)/shard_map/pack_integrals/pallas_call | solution.py:63
  2.1 1.6 %collective-permute-start.7 = (bf16[128,1280]{1,0:T(8,128)(2,1)S(1)}, bf16[128,1280]{1,0:T(8,128)(2,1)S(1)}, u32[]{:S(2)}, u32[]{:S(2)}) collective-permute-start(bf16[128,1280]{1,0:T(8,128)(2,1)S(1)} %get-tuple-element.91.rest_0_), channel_id=1, source_target_pairs={{0,64},{64,128},{128,192},{192,0},{1,65},{65,129},{129,193},{193,1... | collective-permute-start | bytes 983048 | tf_op jit(solution)/shard_map/ppermute | solution.py:23
  3.6 0.8 %collective-permute-start.8 = (bf16[128,1280]{1,0:T(8,128)(2,1)S(1)}, bf16[128,1280]{1,0:T(8,128)(2,1)S(1)}, u32[]{:S(2)}, u32[]{:S(2)}) collective-permute-start(bf16[128,1280]{1,0:T(8,128)(2,1)S(1)} %get-tuple-element.91.rest_0_), channel_id=1, source_target_pairs={{0,32},{32,0},{1,33},{33,1},{2,34},{34,2},{3,35},{35,3},{4,36},{36... | collective-permute-start | bytes 983048 | tf_op jit(solution)/shard_map/ppermute | solution.py:23
  4.4 2.4 %collective-permute-start.9 = (bf16[128,1280]{1,0:T(8,128)(2,1)S(1)}, bf16[128,1280]{1,0:T(8,128)(2,1)S(1)}, u32[]{:S(2)}, u32[]{:S(2)}) collective-permute-start(bf16[128,1280]{1,0:T(8,128)(2,1)S(1)} %get-tuple-element.91.rest_0_), channel_id=1, source_target_pairs={{0,128},{64,192},{128,0},{192,64},{1,129},{65,193},{129,1},{193,65... | collective-permute-start | bytes 983048 | tf_op jit(solution)/shard_map/ppermute | solution.py:23
  6.8 1.4 %collective-permute-start.10 = (bf16[128,1280]{1,0:T(8,128)(2,1)S(1)}, bf16[128,1280]{1,0:T(8,128)(2,1)S(1)}, u32[]{:S(2)}, u32[]{:S(2)}) collective-permute-start(bf16[128,1280]{1,0:T(8,128)(2,1)S(1)} %get-tuple-element.91.rest_0_), channel_id=1, source_target_pairs={{0,192},{64,0},{128,64},{192,128},{1,193},{65,1},{129,65},{193,129... | collective-permute-start | bytes 983048 | tf_op jit(solution)/shard_map/ppermute | solution.py:23
  8.3 3.1 %ranks.1 = (s32[1,512]{1,0:T(1,128)S(1)}, s32[1,512]{1,0:T(1,128)S(1)}, s32[1,1024]{1,0:T(1,128)S(1)}, s32[1]{0:T(128)}) custom-call(s32[3]{0:T(128)S(1)} %pad_add_fusion.where, s32[64]{0:T(128)S(1)} %copy-done.1, s32[8]{0:T(128)S(1)} %copy-done.2, s32[1,64]{1,0:T(1,128)S(1)} %bitcast.51), custom_call_target="tpu_custom_call" | custom-call | flops 3630000128 | tf_op jit(solution)/shard_map/ranks/pallas_call | solution.py:152
  11.4 1.4 %collective-permute-done.8.v.rest_1_ = bf16[128,1280]{1,0:T(8,128)(2,1)S(1)} collective-permute-done((bf16[128,1280]{1,0:T(8,128)(2,1)S(1)}, bf16[128,1280]{1,0:T(8,128)(2,1)S(1)}, u32[]{:S(2)}, u32[]{:S(2)}) %collective-permute-start.8) | collective-permute-done | bytes 327712 | tf_op jit(solution)/shard_map/ppermute | solution.py:23
  14.0 0.7 stack.51.owners
  14.7 1.7 %collective-permute-start.11 = (bf16[128,768]{1,0:T(8,128)(2,1)S(1)}, bf16[128,768]{1,0:T(8,128)(2,1)S(1)}, u32[]{:S(2)}, u32[]{:S(2)}) collective-permute-start(bf16[128,768]{1,0:T(8,128)(2,1)S(1)} %take.6.after), channel_id=1, source_target_pairs={{0,64},{64,128},{128,192},{192,0},{1,65},{65,129},{129,193},{193,1... | collective-permute-start | bytes 589832 | tf_op jit(solution)/shard_map/ppermute | solution.py:23
  16.4 2.4 %collective-permute-start.13 = (bf16[128,768]{1,0:T(8,128)(2,1)S(1)}, bf16[128,768]{1,0:T(8,128)(2,1)S(1)}, u32[]{:S(2)}, u32[]{:S(2)}) collective-permute-start(bf16[128,768]{1,0:T(8,128)(2,1)S(1)} %take.6.after), channel_id=1, source_target_pairs={{0,128},{64,192},{128,0},{192,64},{1,129},{65,193},{129,1},{193,65... | collective-permute-start | bytes 589832 | tf_op jit(solution)/shard_map/ppermute | solution.py:23
  18.8 3.2 %collective-permute-done.9.v.rest_5_ = bf16[128,1280]{1,0:T(8,128)(2,1)S(1)} collective-permute-done((bf16[128,1280]{1,0:T(8,128)(2,1)S(1)}, bf16[128,1280]{1,0:T(8,128)(2,1)S(1)}, u32[]{:S(2)}, u32[]{:S(2)}) %collective-permute-start.9) | collective-permute-done | bytes 327712 | tf_op jit(solution)/shard_map/ppermute | solution.py:23
  22.0 0.7 collective-permute-done.10.v.rest_8_
  22.7 1.4 %collective-permute-start.14 = (bf16[128,512]{1,0:T(8,128)(2,1)S(1)}, bf16[128,512]{1,0:T(8,128)(2,1)S(1)}, u32[]{:S(2)}, u32[]{:S(2)}) collective-permute-start(bf16[128,512]{1,0:T(8,128)(2,1)S(1)} %take.8.rest_1_), channel_id=1, source_target_pairs={{0,32},{32,0},{1,33},{33,1},{2,34},{34,2},{3,35},{35,3},{4,36},{36... | collective-permute-start | bytes 393224 | tf_op jit(solution)/shard_map/ppermute | solution.py:23
  24.1 0.7 collective-permute-start.16
  24.9 6.7 %select_amplitudes.3.t = bf16[8,1280,256]{2,1,0:T(8,128)(2,1)S(1)} custom-call(s32[8]{0:T(128)S(1)} %copy-done.2, s32[16]{0:T(128)S(1)} %copy-done.5, s32[1,512]{1,0:T(1,128)S(1)} %get-tuple-element.87.labels, s32[1,512]{1,0:T(1,128)S(1)} %get-tuple-element.88.after.rank, bf16[512,2048]{1,0:T(8,128)(2,1)} %t.1, bf16[128,512]{1,0:T(8,128)(2,1)S(1)} %take.7.rest_0_, ...), custom_call_target="tpu_custom_call" | custom-call | flops 5500000256 | tf_op jit(solution)/shard_map/select_amplitudes/pallas_call | solution.py:214
  31.7 1.6 %product.3 = (f32[8,2,32,256]{3,2,1,0:T(8,128)S(1)}, f32[8,2,32,256]{3,2,1,0:T(8,128)S(1)}, f32[8,128]{1,0:T(8,128)S(1)}) custom-call(s32[3]{0:T(128)S(1)} %copy-done.10, s32[8]{0:T(128)S(1)} %copy-done.8, s32[8]{0:T(128)S(1)} %copy-done.3, bf16[8,1280,256]{2,1,0:T(8,128)(2,1)S(1)} %select_amplitudes.3.t, bf16[128,1280]{1,0:T(8,128)(2,1)S(1)} %get-tuple-element.91.rest_0_, ...), custom_call_target="tpu_custom_call" | custom-call | flops 2750000128 | tf_op jit(solution)/shard_map/product/pallas_call | solution.py:256
  33.6 0.5 collective-permute-start.18
  34.1 1.4 %collective-permute-done.18.b = f32[8,128]{1,0:T(8,128)S(1)} collective-permute-done((f32[8,128]{1,0:T(8,128)S(1)}, f32[8,128]{1,0:T(8,128)S(1)}, u32[]{:S(2)}, u32[]{:S(2)}) %collective-permute-start.18) | collective-permute-done | bytes 4128 | tf_op jit(solution)/shard_map/ppermute | solution.py:23
  35.7 24.2 %all_to_all.24 = f16[16,32,256]{2,1,0:T(8,128)(2,1)S(1)} all-to-all(f16[16,32,256]{2,1,0:T(8,128)(2,1)S(1)} %convert_element_type.32), channel_id=1, replica_groups=mesh['x'=4,'yl'=2,'vir'=8,'yh'=2,'core'=2] {'vir','yh'}, dimensions={0} | all-to-all | bytes 524288 | tf_op jit(solution)/shard_map/all_to_all | solution.py:465
  59.9 1.7 %spread.1 = (f32[32,512]{1,0:T(8,128)S(1)}, f32[8,32,128]{2,1,0:T(8,128)}) custom-call(s32[3]{0:T(128)S(1)} %copy-done.11, s32[8]{0:T(128)S(1)} %copy-done.4, s32[1,512]{1,0:T(1,128)S(1)} %copy-done.17, s32[1,512]{1,0:T(1,128)S(1)} %get-tuple-element.88.after.rank, s32[1,1024]{1,0:T(1,128)S(1)} %get-tuple-element.89.spots, ...), custom_call_target="tpu_custom_call" | custom-call | flops 1870000000 | tf_op jit(solution)/shard_map/spread/pallas_call | solution.py:329
  61.6 6.5 %all-to-all-start.4 = ((f32[8,32,128]{2,1,0:T(8,128)}), f32[8,32,128]{2,1,0:T(8,128)S(1)}, u32[]{:S(2)}, u32[]{:S(2)}) async-start(f32[8,32,128]{2,1,0:T(8,128)} %get-tuple-element.99), calls=%async_computation.4 | async-start | bytes 262144 | tf_op jit(solution)/shard_map/all_to_all | solution.py:467
  68.9 4.7 %all-to-all-done.4 = f32[8,32,128]{2,1,0:T(8,128)S(1)} async-done(((f32[8,32,128]{2,1,0:T(8,128)}), f32[8,32,128]{2,1,0:T(8,128)S(1)}, u32[]{:S(2)}, u32[]{:S(2)}) %all-to-all-start.4) | async-done | bytes 131104 | tf_op jit(solution)/shard_map/all_to_all | solution.py:467
  73.6 0.4 conditional.3
  74.1 0.6 copy-done.14
  (52 shorter events, 1.7 us)
Async XLA Ops:
  0.0 8.3 %copy-start.2 = (s32[8]{0:T(128)S(1)}, s32[8]{0:T(128)}, u32[]{:S(2)}) copy-start(s32[8]{0:T(128)} %ab.9) | copy-start | bytes 100
  0.0 8.3 %copy-start.1 = (s32[64]{0:T(128)S(1)}, s32[64]{0:T(128)}, u32[]{:S(2)}) copy-start(s32[64]{0:T(128)} %occ.1) | copy-start | bytes 772
  0.1 11.3 %copy-start.9 = (s32[3]{0:T(128)}, s32[3]{0:T(128)S(1)}, u32[]{:S(2)}) copy-start(s32[3]{0:T(128)S(1)} %pad_add_fusion.where) | copy-start | bytes 40
  2.1 10.9 %collective-permute-start.7 = (bf16[128,1280]{1,0:T(8,128)(2,1)S(1)}, bf16[128,1280]{1,0:T(8,128)(2,1)S(1)}, u32[]{:S(2)}, u32[]{:S(2)}) collective-permute-start(bf16[128,1280]{1,0:T(8,128)(2,1)S(1)} %get-tuple-element.91.rest_0_), channel_id=1, source_target_pairs={{0,64},{64,128},{128,192},{192,0},{1,65},{65,129},{129,193},{193,1... | collective-permute-start | bytes 983048 | tf_op jit(solution)/shard_map/ppermute | solution.py:23
  3.6 9.2 %collective-permute-start.8 = (bf16[128,1280]{1,0:T(8,128)(2,1)S(1)}, bf16[128,1280]{1,0:T(8,128)(2,1)S(1)}, u32[]{:S(2)}, u32[]{:S(2)}) collective-permute-start(bf16[128,1280]{1,0:T(8,128)(2,1)S(1)} %get-tuple-element.91.rest_0_), channel_id=1, source_target_pairs={{0,32},{32,0},{1,33},{33,1},{2,34},{34,2},{3,35},{35,3},{4,36},{36... | collective-permute-start | bytes 983048 | tf_op jit(solution)/shard_map/ppermute | solution.py:23
  4.4 17.6 %collective-permute-start.9 = (bf16[128,1280]{1,0:T(8,128)(2,1)S(1)}, bf16[128,1280]{1,0:T(8,128)(2,1)S(1)}, u32[]{:S(2)}, u32[]{:S(2)}) collective-permute-start(bf16[128,1280]{1,0:T(8,128)(2,1)S(1)} %get-tuple-element.91.rest_0_), channel_id=1, source_target_pairs={{0,128},{64,192},{128,0},{192,64},{1,129},{65,193},{129,1},{193,65... | collective-permute-start | bytes 983048 | tf_op jit(solution)/shard_map/ppermute | solution.py:23
  6.8 15.9 %collective-permute-start.10 = (bf16[128,1280]{1,0:T(8,128)(2,1)S(1)}, bf16[128,1280]{1,0:T(8,128)(2,1)S(1)}, u32[]{:S(2)}, u32[]{:S(2)}) collective-permute-start(bf16[128,1280]{1,0:T(8,128)(2,1)S(1)} %get-tuple-element.91.rest_0_), channel_id=1, source_target_pairs={{0,192},{64,0},{128,64},{192,128},{1,193},{65,1},{129,65},{193,129... | collective-permute-start | bytes 983048 | tf_op jit(solution)/shard_map/ppermute | solution.py:23
  8.3 16.6 %copy-start.5 = (s32[16]{0:T(128)S(1)}, s32[16]{0:T(128)}, u32[]{:S(2)}) copy-start(s32[16]{0:T(128)} %cd.3) | copy-start | bytes 196
  11.4 13.5 %copy-start.15 = (s32[1,512]{1,0:T(1,128)}, s32[1,512]{1,0:T(1,128)S(1)}, u32[]{:S(2)}) copy-start(s32[1,512]{1,0:T(1,128)S(1)} %get-tuple-element.87.labels) | copy-start | bytes 6148
  13.0 11.2 %collective-permute-start.12 = (bf16[128,512]{1,0:T(8,128)(2,1)S(1)}, bf16[128,512]{1,0:T(8,128)(2,1)S(1)}, u32[]{:S(2)}, u32[]{:S(2)}) collective-permute-start(bf16[128,512]{1,0:T(8,128)(2,1)S(1)} %take.7.rest_0_), channel_id=1, source_target_pairs={{0,32},{32,0},{1,33},{33,1},{2,34},{34,2},{3,35},{35,3},{4,36},{36... | collective-permute-start | bytes 393224 | tf_op jit(solution)/shard_map/ppermute | solution.py:23
  14.7 16.9 %collective-permute-start.11 = (bf16[128,768]{1,0:T(8,128)(2,1)S(1)}, bf16[128,768]{1,0:T(8,128)(2,1)S(1)}, u32[]{:S(2)}, u32[]{:S(2)}) collective-permute-start(bf16[128,768]{1,0:T(8,128)(2,1)S(1)} %take.6.after), channel_id=1, source_target_pairs={{0,64},{64,128},{128,192},{192,0},{1,65},{65,129},{129,193},{193,1... | collective-permute-start | bytes 589832 | tf_op jit(solution)/shard_map/ppermute | solution.py:23
  16.4 15.3 %collective-permute-start.13 = (bf16[128,768]{1,0:T(8,128)(2,1)S(1)}, bf16[128,768]{1,0:T(8,128)(2,1)S(1)}, u32[]{:S(2)}, u32[]{:S(2)}) collective-permute-start(bf16[128,768]{1,0:T(8,128)(2,1)S(1)} %take.6.after), channel_id=1, source_target_pairs={{0,128},{64,192},{128,0},{192,64},{1,129},{65,193},{129,1},{193,65... | collective-permute-start | bytes 589832 | tf_op jit(solution)/shard_map/ppermute | solution.py:23
  22.0 9.6 %collective-permute-start.15 = (bf16[128,768]{1,0:T(8,128)(2,1)S(1)}, bf16[128,768]{1,0:T(8,128)(2,1)S(1)}, u32[]{:S(2)}, u32[]{:S(2)}) collective-permute-start(bf16[128,768]{1,0:T(8,128)(2,1)S(1)} %take.6.after), channel_id=1, source_target_pairs={{0,192},{64,0},{128,64},{192,128},{1,193},{65,1},{129,65},{193,129... | collective-permute-start | bytes 589832 | tf_op jit(solution)/shard_map/ppermute | solution.py:23
  22.7 8.9 %collective-permute-start.14 = (bf16[128,512]{1,0:T(8,128)(2,1)S(1)}, bf16[128,512]{1,0:T(8,128)(2,1)S(1)}, u32[]{:S(2)}, u32[]{:S(2)}) collective-permute-start(bf16[128,512]{1,0:T(8,128)(2,1)S(1)} %take.8.rest_1_), channel_id=1, source_target_pairs={{0,32},{32,0},{1,33},{33,1},{2,34},{34,2},{3,35},{35,3},{4,36},{36... | collective-permute-start | bytes 393224 | tf_op jit(solution)/shard_map/ppermute | solution.py:23
  24.1 7.5 %collective-permute-start.16 = (bf16[128,512]{1,0:T(8,128)(2,1)S(1)}, bf16[128,512]{1,0:T(8,128)(2,1)S(1)}, u32[]{:S(2)}, u32[]{:S(2)}) collective-permute-start(bf16[128,512]{1,0:T(8,128)(2,1)S(1)} %take.9.rest_2_), channel_id=1, source_target_pairs={{0,32},{32,0},{1,33},{33,1},{2,34},{34,2},{3,35},{35,3},{4,36},{36... | collective-permute-start | bytes 393224 | tf_op jit(solution)/shard_map/ppermute | solution.py:23
  24.9 6.8 %copy-start.8 = (s32[8]{0:T(128)S(1)}, s32[8]{0:T(128)}, u32[]{:S(2)}) copy-start(s32[8]{0:T(128)} %stack.51.owners) | copy-start | bytes 100
  24.9 6.8 %copy-start.10 = (s32[3]{0:T(128)S(1)}, s32[3]{0:T(128)}, u32[]{:S(2)}) copy-start(s32[3]{0:T(128)} %copy-done.9) | copy-start | bytes 40
  33.5 26.4 %copy-start.4 = (s32[8]{0:T(128)S(1)}, s32[8]{0:T(128)}, u32[]{:S(2)}) copy-start(s32[8]{0:T(128)} %ab.9) | copy-start | bytes 100
  33.5 26.4 %copy-start.11 = (s32[3]{0:T(128)S(1)}, s32[3]{0:T(128)}, u32[]{:S(2)}) copy-start(s32[3]{0:T(128)} %copy-done.9) | copy-start | bytes 40
  33.5 26.4 %copy-start.17 = (s32[1,512]{1,0:T(1,128)S(1)}, s32[1,512]{1,0:T(1,128)}, u32[]{:S(2)}) copy-start(s32[1,512]{1,0:T(1,128)} %copy-done.15) | copy-start | bytes 6148
  33.5 2.0 %collective-permute-start.17 = (f32[8,2,32,256]{3,2,1,0:T(8,128)S(1)}, f32[8,2,32,256]{3,2,1,0:T(8,128)S(1)}, u32[]{:S(2)}, u32[]{:S(2)}) collective-permute-start(f32[8,2,32,256]{3,2,1,0:T(8,128)S(1)} %get-tuple-element.96), channel_id=1, source_target_pairs={{0,1},{1,0},{2,3},{3,2},{4,5},{5,4},{6,7},{7,6},{8,9},{9,8},{10,11... | collective-permute-start | bytes 1572872 | tf_op jit(solution)/shard_map/ppermute | solution.py:23
  33.6 1.9 %collective-permute-start.18 = (f32[8,128]{1,0:T(8,128)S(1)}, f32[8,128]{1,0:T(8,128)S(1)}, u32[]{:S(2)}, u32[]{:S(2)}) collective-permute-start(f32[8,128]{1,0:T(8,128)S(1)} %get-tuple-element.97.a), channel_id=1, source_target_pairs={{0,1},{1,0},{2,3},{3,2},{4,5},{5,4},{6,7},{7,6},{8,9},{9,8},{10,11... | collective-permute-start | bytes 12296 | tf_op jit(solution)/shard_map/ppermute | solution.py:23
  35.7 37.9 %copy-start.7 = (s32[16]{0:T(128)S(1)}, s32[16]{0:T(128)}, u32[]{:S(2)}) copy-start(s32[16]{0:T(128)} %cd.3) | copy-start | bytes 196
  61.6 12.0 %all-to-all-start.4 = ((f32[8,32,128]{2,1,0:T(8,128)}), f32[8,32,128]{2,1,0:T(8,128)S(1)}, u32[]{:S(2)}, u32[]{:S(2)}) async-start(f32[8,32,128]{2,1,0:T(8,128)} %get-tuple-element.99), calls=%async_computation.4 | async-start | bytes 262144 | tf_op jit(solution)/shard_map/all_to_all | solution.py:467
  (5 other events, 12.6 us)

commit v3 on v2

--- a/solution.py
+++ b/solution.py
@@ -11,8 +11,7 @@
 ROWS = 256
 SCALES = 8
 STEP = 2.0**14
-FIRST = 10
-DIRECT = 6
+FIRST = (6, 4)
 MIB = 1 << 20
 SMEM = pl.BlockSpec(memory_space=pltpu.SMEM)
 VMEM = pl.BlockSpec(memory_space=pltpu.VMEM)
@@ -31,8 +30,8 @@
     return pltpu.CompilerParams(vmem_limit_bytes=mib * MIB)
 
 
-def pack_kernel(skip, where, ab, cd, v, more, out, count):
-    slots = out.shape[1] // TILE
+def pack_kernel(skip, where, ab, cd, v, more, *rest):
+    outs, count = rest[:-1], rest[-1]
     mine = ab[where[0]]
     for c in range(count.shape[0]):
         count[c] = 0
@@ -43,31 +42,42 @@
         slot = count[label] - skip
         count[label] = count[label] + 1
 
-        @pl.when((label == mine) & (slot >= 0) & (slot < slots))
+        @pl.when(label == mine)
         def _():
-            out[:, pl.ds(pl.multiple_of(slot * TILE, TILE), TILE)] = v[
-                :, pl.ds(pl.multiple_of(t * TILE, TILE), TILE)
-            ]
-
-    @pl.loop(jnp.clip(count[mine] - skip, 0, slots), slots)
-    def _(slot):
-        out[:, pl.ds(pl.multiple_of(slot * TILE, TILE), TILE)] = jnp.zeros((v.shape[0], TILE), v.dtype)
-
+            tile = v[:, pl.ds(pl.multiple_of(t * TILE, TILE), TILE)]
+            first = 0
+            for out in outs:
+                place = slot - first
+                slots = out.shape[1] // TILE
+
+                @pl.when((place >= 0) & (place < slots))
+                def _():
+                    out[:, pl.ds(pl.multiple_of(place * TILE, TILE), TILE)] = tile
+
+                first += slots
+
+    first = skip
+    for out in outs:
+        slots = out.shape[1] // TILE
+
+        @pl.loop(jnp.clip(count[mine] - first, 0, slots), slots)
+        def _(slot):
+            out[:, pl.ds(pl.multiple_of(slot * TILE, TILE), TILE)] = jnp.zeros((v.shape[0], TILE), v.dtype)
+
+        first += slots
     most = count[ab[0]]
     for a in range(1, ab.shape[0]):
         most = jnp.maximum(most, count[ab[a]])
-    more[0] = (most > skip + slots).astype(jnp.int32)
-
-
-def pack(skip, slots, where, ab, cd, v):
+    more[0] = (most > first).astype(jnp.int32)
+
+
+def pack(skip, pieces, where, ab, cd, v):
     return pl.pallas_call(
         functools.partial(pack_kernel, skip),
-        out_shape=[
-            jax.ShapeDtypeStruct((1,), jnp.int32),
-            jax.ShapeDtypeStruct((v.shape[0], slots * TILE), v.dtype),
-        ],
+        out_shape=[jax.ShapeDtypeStruct((1,), jnp.int32)]
+        + [jax.ShapeDtypeStruct((v.shape[0], slots * TILE), v.dtype) for slots in pieces],
         in_specs=[SMEM, SMEM, SMEM, VMEM],
-        out_specs=[SMEM, VMEM],
+        out_specs=[SMEM] + [VMEM] * len(pieces),
         scratch_shapes=[pltpu.SMEM((8,), jnp.int32)],
         compiler_params=params(4),
         cost_estimate=cost(2.0),
@@ -80,7 +90,8 @@
     return match.astype(jnp.float32).astype(jnp.bfloat16)
 
 
-def rank_kernel(where, occ, ab, occ_row, labels, rank, spots, over):
+def rank_kernel(after, where, occ, ab, occ_row, *rest):
+    labels, rank, spots, over = rest[after:]
     orbitals, rows = occ_row.shape[1], labels.shape[1]
     local = rows // orbitals
     irreps, abt = 8, ab.shape[0]
@@ -148,21 +159,21 @@
         )
 
 
-def ranks(where, occ, ab, rows, groups):
-    return pl.pallas_call(
-        rank_kernel,
+def ranks(where, occ, ab, rows, groups, after):
+    return pl.pallas_call(
+        functools.partial(rank_kernel, len(after)),
         out_shape=[
             jax.ShapeDtypeStruct((1, rows), jnp.int32),
             jax.ShapeDtypeStruct((1, rows), jnp.int32),
             jax.ShapeDtypeStruct((1, groups * TILE), jnp.int32),
             jax.ShapeDtypeStruct((1,), jnp.int32),
         ],
-        in_specs=[SMEM, SMEM, SMEM, VMEM],
+        in_specs=[SMEM, SMEM, SMEM, VMEM] + [ANY] * len(after),
         out_specs=[VMEM, VMEM, VMEM, SMEM],
         compiler_params=params(4),
         cost_estimate=cost(3.3),
         name="ranks",
-    )(where, occ, ab, occ.reshape(1, -1))
+    )(where, occ, ab, occ.reshape(1, -1), *after)
 
 
 def select_kernel(skip, after, ab, cd, labels, rank, t, *rest):
@@ -186,16 +197,18 @@
             hot[...] = one_hot(hot.shape, jnp.where(labels[...] == want, rank[...], -1))
             used = jnp.clip(count[want] - skip, 0, slots)
 
-            @pl.loop(0, used)
+            @pl.loop(0, (used + 1) // 2)
             def _(s):
-                i = tile_of[want * tiles + skip + s]
-                piece = t[:, pl.ds(pl.multiple_of(i * TILE, TILE), TILE)]
-                rows_in = jnp.dot(hot[...], piece, preferred_element_type=jnp.float32)
-                out[v, pl.ds(pl.multiple_of(s * TILE, TILE), TILE), :] = jnp.transpose(rows_in).astype(
-                    jnp.bfloat16
-                )
-
-            @pl.loop(used, slots)
+                spans = []
+                for k in range(2):
+                    i = tile_of[jnp.minimum(want * tiles + skip + 2 * s + k, want * tiles + skip + used - 1)]
+                    spans.append(t[:, pl.ds(pl.multiple_of(i * TILE, TILE), TILE)])
+                rows_in = jnp.dot(hot[...], jnp.concatenate(spans, axis=1), preferred_element_type=jnp.float32)
+                out[v, pl.ds(pl.multiple_of(s * 2 * TILE, 2 * TILE), 2 * TILE), :] = jnp.transpose(
+                    rows_in
+                ).astype(jnp.bfloat16)
+
+            @pl.loop(2 * ((used + 1) // 2), slots)
             def _(s):
                 out[v, pl.ds(pl.multiple_of(s * TILE, TILE), TILE), :] = jnp.zeros(
                     (TILE, out.shape[2]), jnp.bfloat16
@@ -222,47 +235,56 @@
             pltpu.SMEM((8,), jnp.int32),
         ],
         compiler_params=params(12),
-        cost_estimate=cost(5.0),
+        cost_estimate=cost(12.0),
         name="select_amplitudes",
     )(ab, cd, labels, rank, t, *after)
 
 
-def product_kernel(sizes, where, owners, ab, t, *rest):
-    pieces, (keep, send, largest, acc) = list(rest[:-4]), rest[-4:]
-    core = where[2]
+def product_kernel(blocks, nx, ny, where, ab, t, *rest):
+    arrays, (keep, send, largest, acc) = rest[:-4], rest[-4:]
+    x, y, core = where[0] // ny, where[0] % ny, where[2]
     part = acc.shape[0] // 4
     most = jnp.zeros((8, acc.shape[1]), jnp.float32)
-    for b, size in enumerate(sizes):
-        v = owners[b]
+    for b, block in enumerate(blocks):
+        v = ((x + nx - b // 2) % nx) * ny + (y + b) % ny
         f = first_of(ab, v)
         first = 0
-        for k in range(size):
-            piece = pieces.pop(0)
-            last = first + piece.shape[1]
-            x = jnp.dot(piece[...], t[f, first:last, :], preferred_element_type=jnp.float32)
-            acc[...] = x if k == 0 else acc[...] + x
+        for n, column, width in block:
+            last = first + width
+            p = jnp.dot(
+                arrays[n][:, column : column + width],
+                t[f, first:last, :],
+                preferred_element_type=jnp.float32,
+            )
+            acc[...] = p if first == 0 else acc[...] + p
             first = last
         most = jnp.maximum(most, jnp.max(jnp.abs(acc[...]).reshape(-1, 8, acc.shape[1]), axis=0))
-        for y in range(2):
+        for half in range(2):
             for out, c in ((keep, core), (send, 1 - core)):
-                row = pl.multiple_of((2 * y + c) * part, part)
-                out[v, y] = acc[pl.ds(row, part), :]
+                row = pl.multiple_of((2 * half + c) * part, part)
+                out[v, half] = acc[pl.ds(row, part), :]
     largest[...] = jnp.full(largest.shape, jnp.max(most), jnp.float32)
 
 
-def product(where, owners, ab, t, blocks):
+def product(where, ab, t, blocks):
     shape = jax.ShapeDtypeStruct((t.shape[0], 2, TILE // 4, t.shape[2]), jnp.float32)
-    pieces = [piece for block in blocks for piece in block]
-    return pl.pallas_call(
-        functools.partial(product_kernel, [len(block) for block in blocks]),
+    arrays, places = [], []
+    for block in blocks:
+        places.append([])
+        for v, column, width in block:
+            if not any(v is a for a in arrays):
+                arrays.append(v)
+            places[-1].append(([v is a for a in arrays].index(True), column, width))
+    return pl.pallas_call(
+        functools.partial(product_kernel, places, lax.axis_size("x"), lax.axis_size("yl")),
         out_shape=[shape, shape, jax.ShapeDtypeStruct((8, TILE), jnp.float32)],
-        in_specs=[SMEM] * 3 + [VMEM] * (1 + len(pieces)),
+        in_specs=[SMEM] * 2 + [VMEM] * (1 + len(arrays)),
         out_specs=[VMEM, VMEM, VMEM],
         scratch_shapes=[pltpu.VMEM((TILE, t.shape[2]), jnp.float32)],
         compiler_params=params(12),
-        cost_estimate=cost(2.5),
+        cost_estimate=cost(1.6),
         name="product",
-    )(where, owners, ab, t, *pieces)
+    )(where, ab, t, *arrays)
 
 
 def combine_kernel(keep, got, a, b, out):
@@ -365,47 +387,54 @@
     )(own, got)
 
 
-def take_kernel(first, v, after, out):
-    out[...] = v[:, first : first + out.shape[1]]
-
-
-def take(v, first, last, after):
-    return pl.pallas_call(
-        functools.partial(take_kernel, first),
-        out_shape=jax.ShapeDtypeStruct((v.shape[0], last - first), v.dtype),
-        in_specs=[VMEM, ANY],
+def join_kernel(after, *refs):
+    ins, out = refs[after:-1], refs[-1]
+    first = 0
+    for v in ins:
+        out[:, first : first + v.shape[1]] = v[...]
+        first += v.shape[1]
+
+
+def join(blocks, after):
+    return pl.pallas_call(
+        functools.partial(join_kernel, len(after)),
+        out_shape=jax.ShapeDtypeStruct(
+            (blocks[0].shape[0], sum(v.shape[1] for v in blocks)), blocks[0].dtype
+        ),
+        in_specs=[ANY] * len(after) + [VMEM] * len(blocks),
         out_specs=VMEM,
-        compiler_params=params(4),
-        name="take",
-    )(v, after)
-
-
-def gather(v, direct, after):
+        compiler_params=params(6),
+        cost_estimate=cost(0.4),
+        name="join",
+    )(*after, *blocks)
+
+
+def gather(pieces):
     nx, ny = lax.axis_size("x"), lax.axis_size("yl")
     swap = shifted("yl", ny, 1)
-    moves = [shifted("x", nx, step) for step in range(1, nx)]
-    partner = swap(v)
-    own = [move(v) for move in moves]
-    head = take(partner, 0, direct * TILE, after)
-    blocks = [[v], [partner]]
-    for move, block in zip(moves, own, strict=True):
-        blocks += [[block], [move(head)]]
-    tails = []
-    if direct * TILE < v.shape[1]:
-        for k, block in enumerate(own):
-            tails.append(take(block, direct * TILE, v.shape[1], head))
-            blocks[2 * k + 3].append(swap(tails[-1]))
-    return blocks, tails
-
-
-def owners_of():
-    nx, ny = lax.axis_size("x"), lax.axis_size("yl")
-    x, y = lax.axis_index("x"), lax.axis_index("yl")
-    owners = []
-    for step in range(nx):
-        first = ((x - step) % nx) * ny
-        owners += [first + y, first + 1 - y]
-    return jnp.stack(owners).astype(jnp.int32)
+    up, down = shifted("x", nx, 1), shifted("x", nx, nx - 1)
+    first, rest = pieces[0], pieces[1:]
+    width = first.shape[1]
+    partner = swap(first)
+    early = [[shifted("x", nx, step)(v) for v in rest] for step in range(1, nx)]
+    mine = {1: up(first), nx - 1: down(first)}
+    other = {1: up(partner), nx - 1: down(partner)}
+    for step in range(2, nx - 1):
+        mine[step] = up(mine[step - 1])
+        other[nx - step] = down(other[nx - step + 1])
+    blocks = [[(first, 0, width)], [(partner, 0, width)]]
+    for step in range(1, nx):
+        blocks += [[(mine[step], 0, width)], [(other[step], 0, width)]]
+    passed = []
+    if rest:
+        through = [rest[0]] + [v[0] for v in early]
+        passed = [join(through, [partner])]
+        back = swap(passed[0])
+        step = rest[0].shape[1]
+        for k, v in enumerate(through):
+            blocks[2 * k].append((v, 0, step))
+            blocks[2 * k + 1].append((back, k * step, step))
+    return blocks, passed
 
 
 def dense(amplitudes, integrals, occ_irrep, ab_irrep, cd_irrep):
@@ -439,22 +468,22 @@
     rows = amplitudes.shape[0]
     me = lax.axis_index("x") * lax.axis_size("yl") + lax.axis_index("yl")
     where = jnp.stack([me, lax.axis_index("vir"), lax.axis_index("core")]).astype(jnp.int32)
-    owners = owners_of()
     tiles = cd_irrep.shape[0]
 
-    def partial_sums(skip, slots, direct, found, packed):
-        blocks, tails = gather(packed, direct, found[1])
-        selected = select(skip, slots, ab_irrep, cd_irrep, *found[:2], amplitudes, tails)
-        return product(where, owners, ab_irrep, selected, blocks)
-
-    more, packed = pack(0, FIRST, where, ab_irrep, cd_irrep, integrals)
-    found = ranks(where, occ_irrep, ab_irrep, rows, groups)
-    sums = partial_sums(0, FIRST, DIRECT, found, packed)
+    def partial_sums(skip, slots, found, blocks, passed):
+        selected = select(skip, slots, ab_irrep, cd_irrep, *found[:2], amplitudes, passed)
+        return product(where, ab_irrep, selected, blocks)
+
+    done = sum(FIRST)
+    more, *packed = pack(0, FIRST, where, ab_irrep, cd_irrep, integrals)
+    blocks, passed = gather(packed)
+    found = ranks(where, occ_irrep, ab_irrep, rows, groups, [])
+    sums = partial_sums(0, done, found, blocks, passed)
 
     def rest(sums, v, found):
-        _, packed = pack(FIRST, tiles - FIRST, where, ab_irrep, cd_irrep, v)
-        added = partial_sums(FIRST, tiles - FIRST, tiles - FIRST, found, packed)
-        return jax.tree.map(jnp.add, list(sums), list(added))
+        _, packed = pack(done, (tiles - done,), where, ab_irrep, cd_irrep, v)
+        blocks, _ = gather([packed])
+        return jax.tree.map(jnp.add, list(sums), list(partial_sums(done, tiles - done, found, blocks, [])))
 
     keep, send, largest = lax.cond(
         more[0] > 0, rest, lambda sums, v, found: list(sums), list(sums), integrals, found

time: 74.6 us -> 69.8 us (0.936)
  Pallas kernels: 15.6 us -> 12.6 us
  waiting for transfers between devices: 11.6 us -> 8.69 us
  starting transfers between devices: 20 us -> 21.6 us
    ppermute x12 -> x13, starting transfers between devices: 13.4 us -> 17 us  [shifted(): lax.ppermute(a, axis, [(i, (i + step) % size) for i in range(size)])]
    ppermute x12 -> x13, waiting for transfers between devices: 6.87 us -> 3.9 us  [shifted(): lax.ppermute(a, axis, [(i, (i + step) % size) for i in range(size)])]
    pallas_call x1, Pallas kernels: 6.69 us -> 3.73 us  [select(): pl.pallas_call(functools.partial(select_kernel, skip, len(after)), out_sh...]
    all_to_all x1, starting transfers between devices: 6.54 us -> 4.62 us  [per_device(): got = lax.all_to_all(send, ('x', 'yl'), 0, 0, tiled=True)]
    pallas_call x6 -> x3, Pallas kernels: 4.71 us -> 4.69 us  [the longest x1 3.09 us: ranks(): pl.pallas_call(functools.partial(rank_kernel, len(after)), out_shape=[jax...]
  transfers between devices with their start and end apart: 13 -> 14, of which waited for: 6 -> 4; matrix products, arithmetic and copies ran while one was open for 1% -> 0% of each run, Pallas kernels for 13% -> 10%
where the time goes in v3:
time: 69.8 us; the launch traced here: 69.5 us
  blocking collectives  24.1 us (35%)
  starting transfers between devices  21.6 us (31%)
  Pallas kernels  12.6 us (18%)
  waiting for transfers between devices  8.69 us (12%)
  between operations  1.48 us (2%)
    all_to_all x1, blocking collectives, per_device(): lax.all_to_all(part, ('vir', 'yh'), 0, 0, tiled=True).astype(jnp.float32)  24.1 us
    ppermute x13, starting transfers between devices, shifted(): lax.ppermute(a, axis, [(i, (i + step) % size) for i in range(size)])  17 us
    all_to_all x1, waiting for transfers between devices, per_device(): got = lax.all_to_all(send, ('x', 'yl'), 0, 0, tiled=True)  4.79 us
    all_to_all x1, starting transfers between devices, per_device(): got = lax.all_to_all(send, ('x', 'yl'), 0, 0, tiled=True)  4.62 us
    ppermute x13, waiting for transfers between devices, shifted(): lax.ppermute(a, axis, [(i, (i + step) % size) for i in range(size)])  3.9 us
    pallas_call x1, Pallas kernels, select(): pl.pallas_call(functools.partial(select_kernel, skip, len(after)), out_sh...  3.73 us
    pallas_call x1, Pallas kernels, ranks(): pl.pallas_call(functools.partial(rank_kernel, len(after)), out_shape=[jax...  3.09 us
    pallas_call x1, Pallas kernels, pack(): pl.pallas_call(functools.partial(pack_kernel, skip), out_shape=[jax.Shape...  1.97 us
  transfers between devices with their start and end apart: 14, of which 4 were waited for; matrix products, arithmetic and copies ran while one was open for 0% of the time, Pallas kernels for 10%

profile of v3, /device:TPU:8, one launch (start us, length us, event | category | flops | bytes accessed | tf_op | source)
XLA Modules:
  0.0 69.5 jit_solution(15142998764377722537)
XLA Ops:
  0.1 2.0 %pack_integrals.3 = (s32[1]{0:T(128)}, bf16[128,768]{1,0:T(8,128)(2,1)S(1)}, bf16[128,512]{1,0:T(8,128)(2,1)S(1)}) custom-call(s32[3]{0:T(128)S(1)} %pad_add_fusion.where, s32[8]{0:T(128)} %ab.9, s32[16]{0:T(128)} %cd.3, bf16[128,2048]{1,0:T(8,128)(2,1)} %v.1), custom_call_target="tpu_custom_call" | custom-call | flops 2200000000 | tf_op jit(solution)/shard_map/pack_integrals/pallas_call | solution.py:75
  2.1 2.2 %collective-permute-start.7 = (bf16[128,768]{1,0:T(8,128)(2,1)S(1)}, bf16[128,768]{1,0:T(8,128)(2,1)S(1)}, u32[]{:S(2)}, u32[]{:S(2)}) collective-permute-start(bf16[128,768]{1,0:T(8,128)(2,1)S(1)} %get-tuple-element.89.rest_0_), channel_id=1, source_target_pairs={{0,32},{32,0},{1,33},{33,1},{2,34},{34,2},{3,35},{35,3},{4,36},{36... | collective-permute-start | bytes 589832 | tf_op jit(solution)/shard_map/ppermute | solution.py:22
  4.3 2.5 %collective-permute-start.9 = (bf16[128,512]{1,0:T(8,128)(2,1)S(1)}, bf16[128,512]{1,0:T(8,128)(2,1)S(1)}, u32[]{:S(2)}, u32[]{:S(2)}) collective-permute-start(bf16[128,512]{1,0:T(8,128)(2,1)S(1)} %get-tuple-element.90.refs_1_.rest_1_), channel_id=1, source_target_pairs={{0,128},{64,192},{128,0},{192,64},{1,129},{65,193},{129,1},{193,65... | collective-permute-start | bytes 393224 | tf_op jit(solution)/shard_map/ppermute | solution.py:22
  6.8 1.4 %collective-permute-start.10 = (bf16[128,512]{1,0:T(8,128)(2,1)S(1)}, bf16[128,512]{1,0:T(8,128)(2,1)S(1)}, u32[]{:S(2)}, u32[]{:S(2)}) collective-permute-start(bf16[128,512]{1,0:T(8,128)(2,1)S(1)} %get-tuple-element.90.refs_1_.rest_1_), channel_id=1, source_target_pairs={{0,192},{64,0},{128,64},{192,128},{1,193},{65,1},{129,65},{193,129... | collective-permute-start | bytes 393224 | tf_op jit(solution)/shard_map/ppermute | solution.py:22
  8.2 0.6 collective-permute-start.12
  8.8 2.7 %collective-permute-start.15 = (bf16[128,768]{1,0:T(8,128)(2,1)S(1)}, bf16[128,768]{1,0:T(8,128)(2,1)S(1)}, u32[]{:S(2)}, u32[]{:S(2)}) collective-permute-start(bf16[128,768]{1,0:T(8,128)(2,1)S(1)} %collective-permute-done.7.refs_0_.rest_2_), channel_id=1, source_target_pairs={{0,192},{64,0},{128,64},{192,128},{1,193},{65,1},{129,65},{193,129... | collective-permute-start | bytes 589832 | tf_op jit(solution)/shard_map/ppermute | solution.py:22
  11.5 3.1 %ranks.1 = (s32[1,512]{1,0:T(1,128)S(1)}, s32[1,512]{1,0:T(1,128)S(1)}, s32[1,1024]{1,0:T(1,128)S(1)}, s32[1]{0:T(128)}) custom-call(s32[3]{0:T(128)S(1)} %pad_add_fusion.where, s32[64]{0:T(128)S(1)} %copy-done.2, s32[8]{0:T(128)S(1)} %copy-done.1, s32[1,64]{1,0:T(1,128)S(1)} %bitcast.43), custom_call_target="tpu_custom_call" | custom-call | flops 3630000128 | tf_op jit(solution)/shard_map/ranks/pallas_call | solution.py:163
  15.3 0.9 %collective-permute-start.17 = (bf16[128,768]{1,0:T(8,128)(2,1)S(1)}, bf16[128,768]{1,0:T(8,128)(2,1)S(1)}, u32[]{:S(2)}, u32[]{:S(2)}) collective-permute-start(bf16[128,768]{1,0:T(8,128)(2,1)S(1)} %get-tuple-element.89.rest_0_), channel_id=1, source_target_pairs={{0,192},{64,0},{128,64},{192,128},{1,193},{65,1},{129,65},{193,129... | collective-permute-start | bytes 589832 | tf_op jit(solution)/shard_map/ppermute | solution.py:22
  16.2 0.8 %collective-permute-start.11 = (bf16[128,2048]{1,0:T(8,128)(2,1)S(1)}, bf16[128,2048]{1,0:T(8,128)(2,1)S(1)}, u32[]{:S(2)}, u32[]{:S(2)}) collective-permute-start(bf16[128,2048]{1,0:T(8,128)(2,1)S(1)} %join.1.rest_0_), channel_id=1, source_target_pairs={{0,32},{32,0},{1,33},{33,1},{2,34},{34,2},{3,35},{35,3},{4,36},{36... | collective-permute-start | bytes 1572872 | tf_op jit(solution)/shard_map/ppermute | solution.py:22
  17.1 2.0 %collective-permute-start.13 = (bf16[128,768]{1,0:T(8,128)(2,1)S(1)}, bf16[128,768]{1,0:T(8,128)(2,1)S(1)}, u32[]{:S(2)}, u32[]{:S(2)}) collective-permute-start(bf16[128,768]{1,0:T(8,128)(2,1)S(1)} %collective-permute-done.7.refs_0_.rest_2_), channel_id=1, source_target_pairs={{0,64},{64,128},{128,192},{192,0},{1,65},{65,129},{129,193},{193,1... | collective-permute-start | bytes 589832 | tf_op jit(solution)/shard_map/ppermute | solution.py:22
  19.1 3.2 %collective-permute-start.16 = (bf16[128,768]{1,0:T(8,128)(2,1)S(1)}, bf16[128,768]{1,0:T(8,128)(2,1)S(1)}, u32[]{:S(2)}, u32[]{:S(2)}) collective-permute-start(bf16[128,768]{1,0:T(8,128)(2,1)S(1)} %collective-permute-done.15.rest_12_), channel_id=1, source_target_pairs={{0,192},{64,0},{128,64},{192,128},{1,193},{65,1},{129,65},{193,129... | collective-permute-start | bytes 589832 | tf_op jit(solution)/shard_map/ppermute | solution.py:22
  22.3 3.7 %select_amplitudes.3.t = bf16[8,1280,256]{2,1,0:T(8,128)(2,1)S(1)} custom-call(s32[8]{0:T(128)S(1)} %copy-done.1, s32[16]{0:T(128)S(1)} %copy-done.3, s32[1,512]{1,0:T(1,128)S(1)} %get-tuple-element.85.labels, s32[1,512]{1,0:T(1,128)S(1)} %get-tuple-element.86.rank, bf16[512,2048]{1,0:T(8,128)(2,1)S(1)} %copy-done.4, bf16[128,2048]{1,0:T(8,128)(2,1)S(1)} %join.1.rest_0_), custom_call_target="tpu_custom_call" | custom-call | flops 13200000000 | tf_op jit(solution)/shard_map/select_amplitudes/pallas_call | solution.py:227
  26.1 1.1 %collective-permute-done.14.rest_7_ = bf16[128,768]{1,0:T(8,128)(2,1)S(1)} collective-permute-done((bf16[128,768]{1,0:T(8,128)(2,1)S(1)}, bf16[128,768]{1,0:T(8,128)(2,1)S(1)}, u32[]{:S(2)}, u32[]{:S(2)}) %collective-permute-start.14) | collective-permute-done | bytes 196640 | tf_op jit(solution)/shard_map/ppermute | solution.py:22
  27.2 1.4 %collective-permute-done.11.rest_3_ = bf16[128,2048]{1,0:T(8,128)(2,1)S(1)} collective-permute-done((bf16[128,2048]{1,0:T(8,128)(2,1)S(1)}, bf16[128,2048]{1,0:T(8,128)(2,1)S(1)}, u32[]{:S(2)}, u32[]{:S(2)}) %collective-permute-start.11) | collective-permute-done | bytes 524320 | tf_op jit(solution)/shard_map/ppermute | solution.py:22
  28.5 1.6 %product.3 = (f32[8,2,32,256]{3,2,1,0:T(8,128)S(1)}, f32[8,2,32,256]{3,2,1,0:T(8,128)S(1)}, f32[8,128]{1,0:T(8,128)S(1)}) custom-call(s32[3]{0:T(128)S(1)} %pad_add_fusion.where, s32[8]{0:T(128)S(1)} %copy-done.1, bf16[8,1280,256]{2,1,0:T(8,128)(2,1)S(1)} %select_amplitudes.3.t, bf16[128,768]{1,0:T(8,128)(2,1)S(1)} %get-tuple-element.89.rest_0_, ...), custom_call_target="tpu_custom_call" | custom-call | flops 1760000000 | tf_op jit(solution)/shard_map/product/pallas_call | solution.py:278
  30.5 0.5 collective-permute-start.19
  31.0 1.4 %collective-permute-done.19.b = f32[8,128]{1,0:T(8,128)S(1)} collective-permute-done((f32[8,128]{1,0:T(8,128)S(1)}, f32[8,128]{1,0:T(8,128)S(1)}, u32[]{:S(2)}, u32[]{:S(2)}) %collective-permute-start.19) | collective-permute-done | bytes 4128 | tf_op jit(solution)/shard_map/ppermute | solution.py:22
  32.5 24.1 %all_to_all.24 = f16[16,32,256]{2,1,0:T(8,128)(2,1)S(1)} all-to-all(f16[16,32,256]{2,1,0:T(8,128)(2,1)S(1)} %convert_element_type.32), channel_id=1, replica_groups=mesh['x'=4,'yl'=2,'vir'=8,'yh'=2,'core'=2] {'vir','yh'}, dimensions={0} | all-to-all | bytes 524288 | tf_op jit(solution)/shard_map/all_to_all | solution.py:494
  56.6 1.7 %spread.1 = (f32[32,512]{1,0:T(8,128)S(1)}, f32[8,32,128]{2,1,0:T(8,128)}) custom-call(s32[3]{0:T(128)S(1)} %pad_add_fusion.where, s32[8]{0:T(128)S(1)} %copy-done.1, s32[1,512]{1,0:T(1,128)S(1)} %get-tuple-element.85.labels, s32[1,512]{1,0:T(1,128)S(1)} %get-tuple-element.86.rank, s32[1,1024]{1,0:T(1,128)S(1)} %get-tuple-element.87.spots, ...), custom_call_target="tpu_custom_call" | custom-call | flops 1870000000 | tf_op jit(solution)/shard_map/spread/pallas_call | solution.py:351
  58.3 4.6 %all-to-all-start.4 = ((f32[8,32,128]{2,1,0:T(8,128)}), f32[8,32,128]{2,1,0:T(8,128)S(1)}, u32[]{:S(2)}, u32[]{:S(2)}) async-start(f32[8,32,128]{2,1,0:T(8,128)} %get-tuple-element.98), calls=%async_computation.4 | async-start | bytes 262144 | tf_op jit(solution)/shard_map/all_to_all | solution.py:496
  63.6 4.8 %all-to-all-done.4 = f32[8,32,128]{2,1,0:T(8,128)S(1)} async-done(((f32[8,32,128]{2,1,0:T(8,128)}), f32[8,32,128]{2,1,0:T(8,128)S(1)}, u32[]{:S(2)}, u32[]{:S(2)}) %all-to-all-start.4) | async-done | bytes 131104 | tf_op jit(solution)/shard_map/all_to_all | solution.py:496
  68.4 0.4 conditional.3
  68.4 0.4 finish.1
  68.9 0.6 copy-done.6
  (32 shorter events, 0.7 us)
Async XLA Ops:
  0.0 11.5 %copy-start.1 = (s32[8]{0:T(128)S(1)}, s32[8]{0:T(128)}, u32[]{:S(2)}) copy-start(s32[8]{0:T(128)} %ab.9) | copy-start | bytes 100
  0.0 11.5 %copy-start.2 = (s32[64]{0:T(128)S(1)}, s32[64]{0:T(128)}, u32[]{:S(2)}) copy-start(s32[64]{0:T(128)} %occ.1) | copy-start | bytes 772
  2.1 6.8 %collective-permute-start.7 = (bf16[128,768]{1,0:T(8,128)(2,1)S(1)}, bf16[128,768]{1,0:T(8,128)(2,1)S(1)}, u32[]{:S(2)}, u32[]{:S(2)}) collective-permute-start(bf16[128,768]{1,0:T(8,128)(2,1)S(1)} %get-tuple-element.89.rest_0_), channel_id=1, source_target_pairs={{0,32},{32,0},{1,33},{33,1},{2,34},{34,2},{3,35},{35,3},{4,36},{36... | collective-permute-start | bytes 589832 | tf_op jit(solution)/shard_map/ppermute | solution.py:22
  4.3 11.0 %collective-permute-start.8 = (bf16[128,512]{1,0:T(8,128)(2,1)S(1)}, bf16[128,512]{1,0:T(8,128)(2,1)S(1)}, u32[]{:S(2)}, u32[]{:S(2)}) collective-permute-start(bf16[128,512]{1,0:T(8,128)(2,1)S(1)} %get-tuple-element.90.refs_1_.rest_1_), channel_id=1, source_target_pairs={{0,64},{64,128},{128,192},{192,0},{1,65},{65,129},{129,193},{193,1... | collective-permute-start | bytes 393224 | tf_op jit(solution)/shard_map/ppermute | solution.py:22
  4.3 11.9 %collective-permute-start.9 = (bf16[128,512]{1,0:T(8,128)(2,1)S(1)}, bf16[128,512]{1,0:T(8,128)(2,1)S(1)}, u32[]{:S(2)}, u32[]{:S(2)}) collective-permute-start(bf16[128,512]{1,0:T(8,128)(2,1)S(1)} %get-tuple-element.90.refs_1_.rest_1_), channel_id=1, source_target_pairs={{0,128},{64,192},{128,0},{192,64},{1,129},{65,193},{129,1},{193,65... | collective-permute-start | bytes 393224 | tf_op jit(solution)/shard_map/ppermute | solution.py:22
  6.8 9.4 %collective-permute-start.10 = (bf16[128,512]{1,0:T(8,128)(2,1)S(1)}, bf16[128,512]{1,0:T(8,128)(2,1)S(1)}, u32[]{:S(2)}, u32[]{:S(2)}) collective-permute-start(bf16[128,512]{1,0:T(8,128)(2,1)S(1)} %get-tuple-element.90.refs_1_.rest_1_), channel_id=1, source_target_pairs={{0,192},{64,0},{128,64},{192,128},{1,193},{65,1},{129,65},{193,129... | collective-permute-start | bytes 393224 | tf_op jit(solution)/shard_map/ppermute | solution.py:22
  8.2 10.9 %collective-permute-start.12 = (bf16[128,768]{1,0:T(8,128)(2,1)S(1)}, bf16[128,768]{1,0:T(8,128)(2,1)S(1)}, u32[]{:S(2)}, u32[]{:S(2)}) collective-permute-start(bf16[128,768]{1,0:T(8,128)(2,1)S(1)} %get-tuple-element.89.rest_0_), channel_id=1, source_target_pairs={{0,64},{64,128},{128,192},{192,0},{1,65},{65,129},{129,193},{193,1... | collective-permute-start | bytes 589832 | tf_op jit(solution)/shard_map/ppermute | solution.py:22
  8.8 10.3 %collective-permute-start.15 = (bf16[128,768]{1,0:T(8,128)(2,1)S(1)}, bf16[128,768]{1,0:T(8,128)(2,1)S(1)}, u32[]{:S(2)}, u32[]{:S(2)}) collective-permute-start(bf16[128,768]{1,0:T(8,128)(2,1)S(1)} %collective-permute-done.7.refs_0_.rest_2_), channel_id=1, source_target_pairs={{0,192},{64,0},{128,64},{192,128},{1,193},{65,1},{129,65},{193,129... | collective-permute-start | bytes 589832 | tf_op jit(solution)/shard_map/ppermute | solution.py:22
  11.5 10.8 %copy-start.3 = (s32[16]{0:T(128)S(1)}, s32[16]{0:T(128)}, u32[]{:S(2)}) copy-start(s32[16]{0:T(128)} %cd.3) | copy-start | bytes 196
  11.5 10.8 %copy-start.4 = (bf16[512,2048]{1,0:T(8,128)(2,1)S(1)}, bf16[512,2048]{1,0:T(8,128)(2,1)}, u32[]{:S(2)}) copy-start(bf16[512,2048]{1,0:T(8,128)(2,1)} %t.1) | copy-start | bytes 6291460
  15.3 10.8 %collective-permute-start.17 = (bf16[128,768]{1,0:T(8,128)(2,1)S(1)}, bf16[128,768]{1,0:T(8,128)(2,1)S(1)}, u32[]{:S(2)}, u32[]{:S(2)}) collective-permute-start(bf16[128,768]{1,0:T(8,128)(2,1)S(1)} %get-tuple-element.89.rest_0_), channel_id=1, source_target_pairs={{0,192},{64,0},{128,64},{192,128},{1,193},{65,1},{129,65},{193,129... | collective-permute-start | bytes 589832 | tf_op jit(solution)/shard_map/ppermute | solution.py:22
  16.2 12.3 %collective-permute-start.11 = (bf16[128,2048]{1,0:T(8,128)(2,1)S(1)}, bf16[128,2048]{1,0:T(8,128)(2,1)S(1)}, u32[]{:S(2)}, u32[]{:S(2)}) collective-permute-start(bf16[128,2048]{1,0:T(8,128)(2,1)S(1)} %join.1.rest_0_), channel_id=1, source_target_pairs={{0,32},{32,0},{1,33},{33,1},{2,34},{34,2},{3,35},{35,3},{4,36},{36... | collective-permute-start | bytes 1572872 | tf_op jit(solution)/shard_map/ppermute | solution.py:22
  17.1 9.0 %collective-permute-start.13 = (bf16[128,768]{1,0:T(8,128)(2,1)S(1)}, bf16[128,768]{1,0:T(8,128)(2,1)S(1)}, u32[]{:S(2)}, u32[]{:S(2)}) collective-permute-start(bf16[128,768]{1,0:T(8,128)(2,1)S(1)} %collective-permute-done.7.refs_0_.rest_2_), channel_id=1, source_target_pairs={{0,64},{64,128},{128,192},{192,0},{1,65},{65,129},{129,193},{193,1... | collective-permute-start | bytes 589832 | tf_op jit(solution)/shard_map/ppermute | solution.py:22
  19.1 8.1 %collective-permute-start.14 = (bf16[128,768]{1,0:T(8,128)(2,1)S(1)}, bf16[128,768]{1,0:T(8,128)(2,1)S(1)}, u32[]{:S(2)}, u32[]{:S(2)}) collective-permute-start(bf16[128,768]{1,0:T(8,128)(2,1)S(1)} %collective-permute-done.12.rest_4_), channel_id=1, source_target_pairs={{0,64},{64,128},{128,192},{192,0},{1,65},{65,129},{129,193},{193,1... | collective-permute-start | bytes 589832 | tf_op jit(solution)/shard_map/ppermute | solution.py:22
  19.1 8.1 %collective-permute-start.16 = (bf16[128,768]{1,0:T(8,128)(2,1)S(1)}, bf16[128,768]{1,0:T(8,128)(2,1)S(1)}, u32[]{:S(2)}, u32[]{:S(2)}) collective-permute-start(bf16[128,768]{1,0:T(8,128)(2,1)S(1)} %collective-permute-done.15.rest_12_), channel_id=1, source_target_pairs={{0,192},{64,0},{128,64},{192,128},{1,193},{65,1},{129,65},{193,129... | collective-permute-start | bytes 589832 | tf_op jit(solution)/shard_map/ppermute | solution.py:22
  26.0 4.1 %copy-start = (bf16[128,2048]{1,0:T(8,128)(2,1)S(1)}, bf16[128,2048]{1,0:T(8,128)(2,1)}, u32[]{:S(2)}) copy-start(bf16[128,2048]{1,0:T(8,128)(2,1)} %v.1) | copy-start | bytes 1572868
  30.4 2.0 %collective-permute-start.18 = (f32[8,2,32,256]{3,2,1,0:T(8,128)S(1)}, f32[8,2,32,256]{3,2,1,0:T(8,128)S(1)}, u32[]{:S(2)}, u32[]{:S(2)}) collective-permute-start(f32[8,2,32,256]{3,2,1,0:T(8,128)S(1)} %get-tuple-element.95), channel_id=1, source_target_pairs={{0,1},{1,0},{2,3},{3,2},{4,5},{5,4},{6,7},{7,6},{8,9},{9,8},{10,11... | collective-permute-start | bytes 1572872 | tf_op jit(solution)/shard_map/ppermute | solution.py:22
  30.5 1.9 %collective-permute-start.19 = (f32[8,128]{1,0:T(8,128)S(1)}, f32[8,128]{1,0:T(8,128)S(1)}, u32[]{:S(2)}, u32[]{:S(2)}) collective-permute-start(f32[8,128]{1,0:T(8,128)S(1)} %get-tuple-element.96.a), channel_id=1, source_target_pairs={{0,1},{1,0},{2,3},{3,2},{4,5},{5,4},{6,7},{7,6},{8,9},{9,8},{10,11... | collective-permute-start | bytes 12296 | tf_op jit(solution)/shard_map/ppermute | solution.py:22
  32.5 35.9 %copy-start.5 = (bf16[512,2048]{1,0:T(8,128)(2,1)S(1)}, bf16[512,2048]{1,0:T(8,128)(2,1)}, u32[]{:S(2)}) copy-start(bf16[512,2048]{1,0:T(8,128)(2,1)} %t.1) | copy-start | bytes 6291460
  58.3 10.1 %all-to-all-start.4 = ((f32[8,32,128]{2,1,0:T(8,128)}), f32[8,32,128]{2,1,0:T(8,128)S(1)}, u32[]{:S(2)}, u32[]{:S(2)}) async-start(f32[8,32,128]{2,1,0:T(8,128)} %get-tuple-element.98), calls=%async_computation.4 | async-start | bytes 262144 | tf_op jit(solution)/shard_map/all_to_all | solution.py:496
  68.8 0.6 copy-start.6

commit v4 on v3

--- a/solution.py
+++ b/solution.py
@@ -11,7 +11,7 @@
 ROWS = 256
 SCALES = 8
 STEP = 2.0**14
-FIRST = (6, 4)
+FIRST = (7, 4)
 MIB = 1 << 20
 SMEM = pl.BlockSpec(memory_space=pltpu.SMEM)
 VMEM = pl.BlockSpec(memory_space=pltpu.VMEM)

time: 69.8 us -> 71.4 us (1.023)
  waiting for transfers between devices: 8.69 us -> 11.5 us
  Pallas kernels: 12.6 us -> 11.3 us
    ppermute x13, waiting for transfers between devices: 3.9 us -> 6.71 us  [shifted(): lax.ppermute(a, axis, [(i, (i + step) % size) for i in range(size)])]
    pallas_call x1, Pallas kernels: 3.73 us -> 2.31 us  [select(): pl.pallas_call(functools.partial(select_kernel, skip, len(after)), out_sh...]
  transfers between devices with their start and end apart: 14 -> 14, of which waited for: 4 -> 6; matrix products, arithmetic and copies ran while one was open for 0% -> 0% of each run, Pallas kernels for 10% -> 8%
where the time goes in v4:
time: 71.4 us; the launch traced here: 71.2 us
  blocking collectives  24.3 us (34%)
  starting transfers between devices  21.6 us (30%)
  waiting for transfers between devices  11.5 us (16%)
  Pallas kernels  11.3 us (16%)
  between operations  1.47 us (2%)
    all_to_all x1, blocking collectives, per_device(): lax.all_to_all(part, ('vir', 'yh'), 0, 0, tiled=True).astype(jnp.float32)  24.3 us
    ppermute x13, starting transfers between devices, shifted(): lax.ppermute(a, axis, [(i, (i + step) % size) for i in range(size)])  16.4 us
    ppermute x13, waiting for transfers between devices, shifted(): lax.ppermute(a, axis, [(i, (i + step) % size) for i in range(size)])  6.71 us
    all_to_all x1, starting transfers between devices, per_device(): got = lax.all_to_all(send, ('x', 'yl'), 0, 0, tiled=True)  5.21 us
    all_to_all x1, waiting for transfers between devices, per_device(): got = lax.all_to_all(send, ('x', 'yl'), 0, 0, tiled=True)  4.79 us
    pallas_call x1, Pallas kernels, ranks(): pl.pallas_call(functools.partial(rank_kernel, len(after)), out_shape=[jax...  3.09 us
    pallas_call x1, Pallas kernels, select(): pl.pallas_call(functools.partial(select_kernel, skip, len(after)), out_sh...  2.31 us
    pallas_call x1, Pallas kernels, pack(): pl.pallas_call(functools.partial(pack_kernel, skip), out_shape=[jax.Shape...  1.93 us
  transfers between devices with their start and end apart: 14, of which 6 were waited for; matrix products, arithmetic and copies ran while one was open for 0% of the time, Pallas kernels for 8%

profile of v4, /device:TPU:8, one launch (start us, length us, event | category | flops | bytes accessed | tf_op | source)
XLA Modules:
  0.0 71.2 jit_solution(65596821568765657)
XLA Ops:
  0.1 1.9 %pack_integrals.3 = (s32[1]{0:T(128)}, bf16[128,896]{1,0:T(8,128)(2,1)S(1)}, bf16[128,512]{1,0:T(8,128)(2,1)S(1)}) custom-call(s32[3]{0:T(128)S(1)} %pad_add_fusion.where, s32[8]{0:T(128)} %ab.9, s32[16]{0:T(128)} %cd.3, bf16[128,2048]{1,0:T(8,128)(2,1)} %v.1), custom_call_target="tpu_custom_call" | custom-call | flops 2200000000 | tf_op jit(solution)/shard_map/pack_integrals/pallas_call | solution.py:75
  2.0 2.3 %collective-permute-start.7 = (bf16[128,896]{1,0:T(8,128)(2,1)S(1)}, bf16[128,896]{1,0:T(8,128)(2,1)S(1)}, u32[]{:S(2)}, u32[]{:S(2)}) collective-permute-start(bf16[128,896]{1,0:T(8,128)(2,1)S(1)} %get-tuple-element.89.rest_0_), channel_id=1, source_target_pairs={{0,32},{32,0},{1,33},{33,1},{2,34},{34,2},{3,35},{35,3},{4,36},{36... | collective-permute-start | bytes 688136 | tf_op jit(solution)/shard_map/ppermute | solution.py:22
  4.3 2.5 %collective-permute-start.9 = (bf16[128,512]{1,0:T(8,128)(2,1)S(1)}, bf16[128,512]{1,0:T(8,128)(2,1)S(1)}, u32[]{:S(2)}, u32[]{:S(2)}) collective-permute-start(bf16[128,512]{1,0:T(8,128)(2,1)S(1)} %get-tuple-element.90.refs_1_.rest_1_), channel_id=1, source_target_pairs={{0,128},{64,192},{128,0},{192,64},{1,129},{65,193},{129,1},{193,65... | collective-permute-start | bytes 393224 | tf_op jit(solution)/shard_map/ppermute | solution.py:22
  6.8 1.4 %collective-permute-start.10 = (bf16[128,512]{1,0:T(8,128)(2,1)S(1)}, bf16[128,512]{1,0:T(8,128)(2,1)S(1)}, u32[]{:S(2)}, u32[]{:S(2)}) collective-permute-start(bf16[128,512]{1,0:T(8,128)(2,1)S(1)} %get-tuple-element.90.refs_1_.rest_1_), channel_id=1, source_target_pairs={{0,192},{64,0},{128,64},{192,128},{1,193},{65,1},{129,65},{193,129... | collective-permute-start | bytes 393224 | tf_op jit(solution)/shard_map/ppermute | solution.py:22
  8.2 0.6 collective-permute-start.12
  8.8 0.7 collective-permute-done.7.refs_0_.rest_2_
  9.5 2.7 %collective-permute-start.15 = (bf16[128,896]{1,0:T(8,128)(2,1)S(1)}, bf16[128,896]{1,0:T(8,128)(2,1)S(1)}, u32[]{:S(2)}, u32[]{:S(2)}) collective-permute-start(bf16[128,896]{1,0:T(8,128)(2,1)S(1)} %collective-permute-done.7.refs_0_.rest_2_), channel_id=1, source_target_pairs={{0,192},{64,0},{128,64},{192,128},{1,193},{65,1},{129,65},{193,129... | collective-permute-start | bytes 688136 | tf_op jit(solution)/shard_map/ppermute | solution.py:22
  12.2 3.1 %ranks.1 = (s32[1,512]{1,0:T(1,128)S(1)}, s32[1,512]{1,0:T(1,128)S(1)}, s32[1,1024]{1,0:T(1,128)S(1)}, s32[1]{0:T(128)}) custom-call(s32[3]{0:T(128)S(1)} %pad_add_fusion.where, s32[64]{0:T(128)S(1)} %copy-done.2, s32[8]{0:T(128)S(1)} %copy-done.1, s32[1,64]{1,0:T(1,128)S(1)} %bitcast.43), custom_call_target="tpu_custom_call" | custom-call | flops 3630000128 | tf_op jit(solution)/shard_map/ranks/pallas_call | solution.py:163
  16.0 0.9 %collective-permute-start.17 = (bf16[128,896]{1,0:T(8,128)(2,1)S(1)}, bf16[128,896]{1,0:T(8,128)(2,1)S(1)}, u32[]{:S(2)}, u32[]{:S(2)}) collective-permute-start(bf16[128,896]{1,0:T(8,128)(2,1)S(1)} %get-tuple-element.89.rest_0_), channel_id=1, source_target_pairs={{0,192},{64,0},{128,64},{192,128},{1,193},{65,1},{129,65},{193,129... | collective-permute-start | bytes 688136 | tf_op jit(solution)/shard_map/ppermute | solution.py:22
  17.0 0.5 collective-permute-start.11
  17.5 1.6 %collective-permute-start.13 = (bf16[128,896]{1,0:T(8,128)(2,1)S(1)}, bf16[128,896]{1,0:T(8,128)(2,1)S(1)}, u32[]{:S(2)}, u32[]{:S(2)}) collective-permute-start(bf16[128,896]{1,0:T(8,128)(2,1)S(1)} %collective-permute-done.7.refs_0_.rest_2_), channel_id=1, source_target_pairs={{0,64},{64,128},{128,192},{192,0},{1,65},{65,129},{129,193},{193,1... | collective-permute-start | bytes 688136 | tf_op jit(solution)/shard_map/ppermute | solution.py:22
  19.1 3.2 %collective-permute-start.16 = (bf16[128,896]{1,0:T(8,128)(2,1)S(1)}, bf16[128,896]{1,0:T(8,128)(2,1)S(1)}, u32[]{:S(2)}, u32[]{:S(2)}) collective-permute-start(bf16[128,896]{1,0:T(8,128)(2,1)S(1)} %collective-permute-done.15.rest_12_), channel_id=1, source_target_pairs={{0,192},{64,0},{128,64},{192,128},{1,193},{65,1},{129,65},{193,129... | collective-permute-start | bytes 688136 | tf_op jit(solution)/shard_map/ppermute | solution.py:22
  22.3 2.3 %select_amplitudes.3.t = bf16[8,1408,256]{2,1,0:T(8,128)(2,1)S(1)} custom-call(s32[8]{0:T(128)S(1)} %copy-done.1, s32[16]{0:T(128)S(1)} %copy-done.3, s32[1,512]{1,0:T(1,128)S(1)} %get-tuple-element.85.labels, s32[1,512]{1,0:T(1,128)S(1)} %get-tuple-element.86.rank, bf16[512,2048]{1,0:T(8,128)(2,1)S(1)} %copy-done.4, bf16[128,2048]{1,0:T(8,128)(2,1)S(1)} %join.1.rest_0_), custom_call_target="tpu_custom_call" | custom-call | flops 13200000000 | tf_op jit(solution)/shard_map/select_amplitudes/pallas_call | solution.py:227
  24.6 2.1 %collective-permute-done.13.rest_6_ = bf16[128,896]{1,0:T(8,128)(2,1)S(1)} collective-permute-done((bf16[128,896]{1,0:T(8,128)(2,1)S(1)}, bf16[128,896]{1,0:T(8,128)(2,1)S(1)}, u32[]{:S(2)}, u32[]{:S(2)}) %collective-permute-start.13) | collective-permute-done | bytes 229408 | tf_op jit(solution)/shard_map/ppermute | solution.py:22
  26.8 2.5 %collective-permute-done.14.rest_7_ = bf16[128,896]{1,0:T(8,128)(2,1)S(1)} collective-permute-done((bf16[128,896]{1,0:T(8,128)(2,1)S(1)}, bf16[128,896]{1,0:T(8,128)(2,1)S(1)}, u32[]{:S(2)}, u32[]{:S(2)}) %collective-permute-start.14) | collective-permute-done | bytes 229408 | tf_op jit(solution)/shard_map/ppermute | solution.py:22
  29.3 1.7 %product.3 = (f32[8,2,32,256]{3,2,1,0:T(8,128)S(1)}, f32[8,2,32,256]{3,2,1,0:T(8,128)S(1)}, f32[8,128]{1,0:T(8,128)S(1)}) custom-call(s32[3]{0:T(128)S(1)} %pad_add_fusion.where, s32[8]{0:T(128)S(1)} %copy-done.1, bf16[8,1408,256]{2,1,0:T(8,128)(2,1)S(1)} %select_amplitudes.3.t, bf16[128,896]{1,0:T(8,128)(2,1)S(1)} %get-tuple-element.89.rest_0_, ...), custom_call_target="tpu_custom_call" | custom-call | flops 1760000000 | tf_op jit(solution)/shard_map/product/pallas_call | solution.py:278
  31.3 0.5 collective-permute-start.19
  31.8 1.4 %collective-permute-done.19.b = f32[8,128]{1,0:T(8,128)S(1)} collective-permute-done((f32[8,128]{1,0:T(8,128)S(1)}, f32[8,128]{1,0:T(8,128)S(1)}, u32[]{:S(2)}, u32[]{:S(2)}) %collective-permute-start.19) | collective-permute-done | bytes 4128 | tf_op jit(solution)/shard_map/ppermute | solution.py:22
  33.4 24.3 %all_to_all.24 = f16[16,32,256]{2,1,0:T(8,128)(2,1)S(1)} all-to-all(f16[16,32,256]{2,1,0:T(8,128)(2,1)S(1)} %convert_element_type.32), channel_id=1, replica_groups=mesh['x'=4,'yl'=2,'vir'=8,'yh'=2,'core'=2] {'vir','yh'}, dimensions={0} | all-to-all | bytes 524288 | tf_op jit(solution)/shard_map/all_to_all | solution.py:494
  57.7 1.7 %spread.1 = (f32[32,512]{1,0:T(8,128)S(1)}, f32[8,32,128]{2,1,0:T(8,128)}) custom-call(s32[3]{0:T(128)S(1)} %pad_add_fusion.where, s32[8]{0:T(128)S(1)} %copy-done.1, s32[1,512]{1,0:T(1,128)S(1)} %get-tuple-element.85.labels, s32[1,512]{1,0:T(1,128)S(1)} %get-tuple-element.86.rank, s32[1,1024]{1,0:T(1,128)S(1)} %get-tuple-element.87.spots, ...), custom_call_target="tpu_custom_call" | custom-call | flops 1870000000 | tf_op jit(solution)/shard_map/spread/pallas_call | solution.py:351
  59.4 5.2 %all-to-all-start.4 = ((f32[8,32,128]{2,1,0:T(8,128)}), f32[8,32,128]{2,1,0:T(8,128)S(1)}, u32[]{:S(2)}, u32[]{:S(2)}) async-start(f32[8,32,128]{2,1,0:T(8,128)} %get-tuple-element.98), calls=%async_computation.4 | async-start | bytes 262144 | tf_op jit(solution)/shard_map/all_to_all | solution.py:496
  65.3 4.8 %all-to-all-done.4 = f32[8,32,128]{2,1,0:T(8,128)S(1)} async-done(((f32[8,32,128]{2,1,0:T(8,128)}), f32[8,32,128]{2,1,0:T(8,128)S(1)}, u32[]{:S(2)}, u32[]{:S(2)}) %all-to-all-start.4) | async-done | bytes 131104 | tf_op jit(solution)/shard_map/all_to_all | solution.py:496
  70.1 0.4 conditional.3
  70.5 0.6 copy-done.6
  (32 shorter events, 1.2 us)
Async XLA Ops:
  0.0 12.2 %copy-start.1 = (s32[8]{0:T(128)S(1)}, s32[8]{0:T(128)}, u32[]{:S(2)}) copy-start(s32[8]{0:T(128)} %ab.9) | copy-start | bytes 100
  0.0 12.2 %copy-start.2 = (s32[64]{0:T(128)S(1)}, s32[64]{0:T(128)}, u32[]{:S(2)}) copy-start(s32[64]{0:T(128)} %occ.1) | copy-start | bytes 772
  2.0 7.4 %collective-permute-start.7 = (bf16[128,896]{1,0:T(8,128)(2,1)S(1)}, bf16[128,896]{1,0:T(8,128)(2,1)S(1)}, u32[]{:S(2)}, u32[]{:S(2)}) collective-permute-start(bf16[128,896]{1,0:T(8,128)(2,1)S(1)} %get-tuple-element.89.rest_0_), channel_id=1, source_target_pairs={{0,32},{32,0},{1,33},{33,1},{2,34},{34,2},{3,35},{35,3},{4,36},{36... | collective-permute-start | bytes 688136 | tf_op jit(solution)/shard_map/ppermute | solution.py:22
  4.3 11.7 %collective-permute-start.8 = (bf16[128,512]{1,0:T(8,128)(2,1)S(1)}, bf16[128,512]{1,0:T(8,128)(2,1)S(1)}, u32[]{:S(2)}, u32[]{:S(2)}) collective-permute-start(bf16[128,512]{1,0:T(8,128)(2,1)S(1)} %get-tuple-element.90.refs_1_.rest_1_), channel_id=1, source_target_pairs={{0,64},{64,128},{128,192},{192,0},{1,65},{65,129},{129,193},{193,1... | collective-permute-start | bytes 393224 | tf_op jit(solution)/shard_map/ppermute | solution.py:22
  4.3 12.6 %collective-permute-start.9 = (bf16[128,512]{1,0:T(8,128)(2,1)S(1)}, bf16[128,512]{1,0:T(8,128)(2,1)S(1)}, u32[]{:S(2)}, u32[]{:S(2)}) collective-permute-start(bf16[128,512]{1,0:T(8,128)(2,1)S(1)} %get-tuple-element.90.refs_1_.rest_1_), channel_id=1, source_target_pairs={{0,128},{64,192},{128,0},{192,64},{1,129},{65,193},{129,1},{193,65... | collective-permute-start | bytes 393224 | tf_op jit(solution)/shard_map/ppermute | solution.py:22
  6.8 10.1 %collective-permute-start.10 = (bf16[128,512]{1,0:T(8,128)(2,1)S(1)}, bf16[128,512]{1,0:T(8,128)(2,1)S(1)}, u32[]{:S(2)}, u32[]{:S(2)}) collective-permute-start(bf16[128,512]{1,0:T(8,128)(2,1)S(1)} %get-tuple-element.90.refs_1_.rest_1_), channel_id=1, source_target_pairs={{0,192},{64,0},{128,64},{192,128},{1,193},{65,1},{129,65},{193,129... | collective-permute-start | bytes 393224 | tf_op jit(solution)/shard_map/ppermute | solution.py:22
  8.2 10.8 %collective-permute-start.12 = (bf16[128,896]{1,0:T(8,128)(2,1)S(1)}, bf16[128,896]{1,0:T(8,128)(2,1)S(1)}, u32[]{:S(2)}, u32[]{:S(2)}) collective-permute-start(bf16[128,896]{1,0:T(8,128)(2,1)S(1)} %get-tuple-element.89.rest_0_), channel_id=1, source_target_pairs={{0,64},{64,128},{128,192},{192,0},{1,65},{65,129},{129,193},{193,1... | collective-permute-start | bytes 688136 | tf_op jit(solution)/shard_map/ppermute | solution.py:22
  9.5 9.6 %collective-permute-start.15 = (bf16[128,896]{1,0:T(8,128)(2,1)S(1)}, bf16[128,896]{1,0:T(8,128)(2,1)S(1)}, u32[]{:S(2)}, u32[]{:S(2)}) collective-permute-start(bf16[128,896]{1,0:T(8,128)(2,1)S(1)} %collective-permute-done.7.refs_0_.rest_2_), channel_id=1, source_target_pairs={{0,192},{64,0},{128,64},{192,128},{1,193},{65,1},{129,65},{193,129... | collective-permute-start | bytes 688136 | tf_op jit(solution)/shard_map/ppermute | solution.py:22
  12.2 10.1 %copy-start.3 = (s32[16]{0:T(128)S(1)}, s32[16]{0:T(128)}, u32[]{:S(2)}) copy-start(s32[16]{0:T(128)} %cd.3) | copy-start | bytes 196
  12.2 10.1 %copy-start.4 = (bf16[512,2048]{1,0:T(8,128)(2,1)S(1)}, bf16[512,2048]{1,0:T(8,128)(2,1)}, u32[]{:S(2)}) copy-start(bf16[512,2048]{1,0:T(8,128)(2,1)} %t.1) | copy-start | bytes 6291460
  16.0 8.6 %collective-permute-start.17 = (bf16[128,896]{1,0:T(8,128)(2,1)S(1)}, bf16[128,896]{1,0:T(8,128)(2,1)S(1)}, u32[]{:S(2)}, u32[]{:S(2)}) collective-permute-start(bf16[128,896]{1,0:T(8,128)(2,1)S(1)} %get-tuple-element.89.rest_0_), channel_id=1, source_target_pairs={{0,192},{64,0},{128,64},{192,128},{1,193},{65,1},{129,65},{193,129... | collective-permute-start | bytes 688136 | tf_op jit(solution)/shard_map/ppermute | solution.py:22
  17.0 12.3 %collective-permute-start.11 = (bf16[128,2048]{1,0:T(8,128)(2,1)S(1)}, bf16[128,2048]{1,0:T(8,128)(2,1)S(1)}, u32[]{:S(2)}, u32[]{:S(2)}) collective-permute-start(bf16[128,2048]{1,0:T(8,128)(2,1)S(1)} %join.1.rest_0_), channel_id=1, source_target_pairs={{0,32},{32,0},{1,33},{33,1},{2,34},{34,2},{3,35},{35,3},{4,36},{36... | collective-permute-start | bytes 1572872 | tf_op jit(solution)/shard_map/ppermute | solution.py:22
  17.5 9.3 %collective-permute-start.13 = (bf16[128,896]{1,0:T(8,128)(2,1)S(1)}, bf16[128,896]{1,0:T(8,128)(2,1)S(1)}, u32[]{:S(2)}, u32[]{:S(2)}) collective-permute-start(bf16[128,896]{1,0:T(8,128)(2,1)S(1)} %collective-permute-done.7.refs_0_.rest_2_), channel_id=1, source_target_pairs={{0,64},{64,128},{128,192},{192,0},{1,65},{65,129},{129,193},{193,1... | collective-permute-start | bytes 688136 | tf_op jit(solution)/shard_map/ppermute | solution.py:22
  19.1 10.2 %collective-permute-start.14 = (bf16[128,896]{1,0:T(8,128)(2,1)S(1)}, bf16[128,896]{1,0:T(8,128)(2,1)S(1)}, u32[]{:S(2)}, u32[]{:S(2)}) collective-permute-start(bf16[128,896]{1,0:T(8,128)(2,1)S(1)} %collective-permute-done.12.rest_4_), channel_id=1, source_target_pairs={{0,64},{64,128},{128,192},{192,0},{1,65},{65,129},{129,193},{193,1... | collective-permute-start | bytes 688136 | tf_op jit(solution)/shard_map/ppermute | solution.py:22
  19.1 10.1 %collective-permute-start.16 = (bf16[128,896]{1,0:T(8,128)(2,1)S(1)}, bf16[128,896]{1,0:T(8,128)(2,1)S(1)}, u32[]{:S(2)}, u32[]{:S(2)}) collective-permute-start(bf16[128,896]{1,0:T(8,128)(2,1)S(1)} %collective-permute-done.15.rest_12_), channel_id=1, source_target_pairs={{0,192},{64,0},{128,64},{192,128},{1,193},{65,1},{129,65},{193,129... | collective-permute-start | bytes 688136 | tf_op jit(solution)/shard_map/ppermute | solution.py:22
  24.6 6.4 %copy-start = (bf16[128,2048]{1,0:T(8,128)(2,1)S(1)}, bf16[128,2048]{1,0:T(8,128)(2,1)}, u32[]{:S(2)}) copy-start(bf16[128,2048]{1,0:T(8,128)(2,1)} %v.1) | copy-start | bytes 1572868
  31.2 2.0 %collective-permute-start.18 = (f32[8,2,32,256]{3,2,1,0:T(8,128)S(1)}, f32[8,2,32,256]{3,2,1,0:T(8,128)S(1)}, u32[]{:S(2)}, u32[]{:S(2)}) collective-permute-start(f32[8,2,32,256]{3,2,1,0:T(8,128)S(1)} %get-tuple-element.95), channel_id=1, source_target_pairs={{0,1},{1,0},{2,3},{3,2},{4,5},{5,4},{6,7},{7,6},{8,9},{9,8},{10,11... | collective-permute-start | bytes 1572872 | tf_op jit(solution)/shard_map/ppermute | solution.py:22
  31.3 1.9 %collective-permute-start.19 = (f32[8,128]{1,0:T(8,128)S(1)}, f32[8,128]{1,0:T(8,128)S(1)}, u32[]{:S(2)}, u32[]{:S(2)}) collective-permute-start(f32[8,128]{1,0:T(8,128)S(1)} %get-tuple-element.96.a), channel_id=1, source_target_pairs={{0,1},{1,0},{2,3},{3,2},{4,5},{5,4},{6,7},{7,6},{8,9},{9,8},{10,11... | collective-permute-start | bytes 12296 | tf_op jit(solution)/shard_map/ppermute | solution.py:22
  33.4 36.7 %copy-start.5 = (bf16[512,2048]{1,0:T(8,128)(2,1)S(1)}, bf16[512,2048]{1,0:T(8,128)(2,1)}, u32[]{:S(2)}) copy-start(bf16[512,2048]{1,0:T(8,128)(2,1)} %t.1) | copy-start | bytes 6291460
  59.4 10.7 %all-to-all-start.4 = ((f32[8,32,128]{2,1,0:T(8,128)}), f32[8,32,128]{2,1,0:T(8,128)S(1)}, u32[]{:S(2)}, u32[]{:S(2)}) async-start(f32[8,32,128]{2,1,0:T(8,128)} %get-tuple-element.98), calls=%async_computation.4 | async-start | bytes 262144 | tf_op jit(solution)/shard_map/all_to_all | solution.py:496
  70.5 0.6 copy-start.6

commit v5 on v4

--- a/solution.py
+++ b/solution.py
@@ -224,9 +224,10 @@
 
 
 def select(skip, slots, ab, cd, labels, rank, t, after):
+    room = slots + slots % 2
     return pl.pallas_call(
         functools.partial(select_kernel, skip, len(after)),
-        out_shape=jax.ShapeDtypeStruct((ab.shape[0], slots * TILE, ROWS), t.dtype),
+        out_shape=jax.ShapeDtypeStruct((ab.shape[0], room * TILE, ROWS), t.dtype),
         in_specs=[SMEM, SMEM, VMEM, VMEM, VMEM] + [ANY] * len(after),
         out_specs=VMEM,
         scratch_shapes=[

time: 71.4 us -> 71.4 us (level)
  Pallas kernels: 11.3 us -> 12.3 us
  waiting for transfers between devices: 11.5 us -> 10.5 us
    ppermute x13, waiting for transfers between devices: 6.71 us -> 5.69 us  [shifted(): lax.ppermute(a, axis, [(i, (i + step) % size) for i in range(size)])]
    pallas_call x1, Pallas kernels: 2.31 us -> 3.3 us  [select(): pl.pallas_call(functools.partial(select_kernel, skip, len(after)), out_sh...]
  transfers between devices with their start and end apart: 14 -> 14, of which waited for: 6 -> 5; matrix products, arithmetic and copies ran while one was open for 0% -> 0% of each run, Pallas kernels for 8% -> 9%
where the time goes in v5:
time: 71.4 us; the launch traced here: 71.2 us
  blocking collectives  24.3 us (34%)
  starting transfers between devices  21.6 us (30%)
  Pallas kernels  12.3 us (17%)
  waiting for transfers between devices  10.5 us (15%)
  between operations  1.47 us (2%)
    all_to_all x1, blocking collectives, per_device(): lax.all_to_all(part, ('vir', 'yh'), 0, 0, tiled=True).astype(jnp.float32)  24.3 us
    ppermute x13, starting transfers between devices, shifted(): lax.ppermute(a, axis, [(i, (i + step) % size) for i in range(size)])  16.4 us
    ppermute x13, waiting for transfers between devices, shifted(): lax.ppermute(a, axis, [(i, (i + step) % size) for i in range(size)])  5.69 us
    all_to_all x1, starting transfers between devices, per_device(): got = lax.all_to_all(send, ('x', 'yl'), 0, 0, tiled=True)  5.18 us
    all_to_all x1, waiting for transfers between devices, per_device(): got = lax.all_to_all(send, ('x', 'yl'), 0, 0, tiled=True)  4.79 us
    pallas_call x1, Pallas kernels, select(): pl.pallas_call(functools.partial(select_kernel, skip, len(after)), out_sh...  3.3 us
    pallas_call x1, Pallas kernels, ranks(): pl.pallas_call(functools.partial(rank_kernel, len(after)), out_shape=[jax...  3.09 us
    pallas_call x1, Pallas kernels, pack(): pl.pallas_call(functools.partial(pack_kernel, skip), out_shape=[jax.Shape...  1.93 us
  transfers between devices with their start and end apart: 14, of which 5 were waited for; matrix products, arithmetic and copies ran while one was open for 0% of the time, Pallas kernels for 9%

profile of v5, /device:TPU:8, one launch (start us, length us, event | category | flops | bytes accessed | tf_op | source)
XLA Modules:
  0.0 71.2 jit_solution(9120224246935158136)
XLA Ops:
  0.1 1.9 %pack_integrals.3 = (s32[1]{0:T(128)}, bf16[128,896]{1,0:T(8,128)(2,1)S(1)}, bf16[128,512]{1,0:T(8,128)(2,1)S(1)}) custom-call(s32[3]{0:T(128)S(1)} %pad_add_fusion.where, s32[8]{0:T(128)} %ab.9, s32[16]{0:T(128)} %cd.3, bf16[128,2048]{1,0:T(8,128)(2,1)} %v.1), custom_call_target="tpu_custom_call" | custom-call | flops 2200000000 | tf_op jit(solution)/shard_map/pack_integrals/pallas_call | solution.py:75
  2.0 2.3 %collective-permute-start.7 = (bf16[128,896]{1,0:T(8,128)(2,1)S(1)}, bf16[128,896]{1,0:T(8,128)(2,1)S(1)}, u32[]{:S(2)}, u32[]{:S(2)}) collective-permute-start(bf16[128,896]{1,0:T(8,128)(2,1)S(1)} %get-tuple-element.89.rest_0_), channel_id=1, source_target_pairs={{0,32},{32,0},{1,33},{33,1},{2,34},{34,2},{3,35},{35,3},{4,36},{36... | collective-permute-start | bytes 688136 | tf_op jit(solution)/shard_map/ppermute | solution.py:22
  4.3 2.5 %collective-permute-start.9 = (bf16[128,512]{1,0:T(8,128)(2,1)S(1)}, bf16[128,512]{1,0:T(8,128)(2,1)S(1)}, u32[]{:S(2)}, u32[]{:S(2)}) collective-permute-start(bf16[128,512]{1,0:T(8,128)(2,1)S(1)} %get-tuple-element.90.refs_1_.rest_1_), channel_id=1, source_target_pairs={{0,128},{64,192},{128,0},{192,64},{1,129},{65,193},{129,1},{193,65... | collective-permute-start | bytes 393224 | tf_op jit(solution)/shard_map/ppermute | solution.py:22
  6.8 1.4 %collective-permute-start.10 = (bf16[128,512]{1,0:T(8,128)(2,1)S(1)}, bf16[128,512]{1,0:T(8,128)(2,1)S(1)}, u32[]{:S(2)}, u32[]{:S(2)}) collective-permute-start(bf16[128,512]{1,0:T(8,128)(2,1)S(1)} %get-tuple-element.90.refs_1_.rest_1_), channel_id=1, source_target_pairs={{0,192},{64,0},{128,64},{192,128},{1,193},{65,1},{129,65},{193,129... | collective-permute-start | bytes 393224 | tf_op jit(solution)/shard_map/ppermute | solution.py:22
  8.2 0.6 collective-permute-start.12
  8.8 0.6 collective-permute-done.7.refs_0_.rest_2_
  9.4 2.8 %collective-permute-start.15 = (bf16[128,896]{1,0:T(8,128)(2,1)S(1)}, bf16[128,896]{1,0:T(8,128)(2,1)S(1)}, u32[]{:S(2)}, u32[]{:S(2)}) collective-permute-start(bf16[128,896]{1,0:T(8,128)(2,1)S(1)} %collective-permute-done.7.refs_0_.rest_2_), channel_id=1, source_target_pairs={{0,192},{64,0},{128,64},{192,128},{1,193},{65,1},{129,65},{193,129... | collective-permute-start | bytes 688136 | tf_op jit(solution)/shard_map/ppermute | solution.py:22
  12.2 3.1 %ranks.1 = (s32[1,512]{1,0:T(1,128)S(1)}, s32[1,512]{1,0:T(1,128)S(1)}, s32[1,1024]{1,0:T(1,128)S(1)}, s32[1]{0:T(128)}) custom-call(s32[3]{0:T(128)S(1)} %pad_add_fusion.where, s32[64]{0:T(128)S(1)} %copy-done.2, s32[8]{0:T(128)S(1)} %copy-done.1, s32[1,64]{1,0:T(1,128)S(1)} %bitcast.43), custom_call_target="tpu_custom_call" | custom-call | flops 3630000128 | tf_op jit(solution)/shard_map/ranks/pallas_call | solution.py:163
  16.0 0.9 %collective-permute-start.17 = (bf16[128,896]{1,0:T(8,128)(2,1)S(1)}, bf16[128,896]{1,0:T(8,128)(2,1)S(1)}, u32[]{:S(2)}, u32[]{:S(2)}) collective-permute-start(bf16[128,896]{1,0:T(8,128)(2,1)S(1)} %get-tuple-element.89.rest_0_), channel_id=1, source_target_pairs={{0,192},{64,0},{128,64},{192,128},{1,193},{65,1},{129,65},{193,129... | collective-permute-start | bytes 688136 | tf_op jit(solution)/shard_map/ppermute | solution.py:22
  17.0 0.5 collective-permute-start.11
  17.5 1.6 %collective-permute-start.13 = (bf16[128,896]{1,0:T(8,128)(2,1)S(1)}, bf16[128,896]{1,0:T(8,128)(2,1)S(1)}, u32[]{:S(2)}, u32[]{:S(2)}) collective-permute-start(bf16[128,896]{1,0:T(8,128)(2,1)S(1)} %collective-permute-done.7.refs_0_.rest_2_), channel_id=1, source_target_pairs={{0,64},{64,128},{128,192},{192,0},{1,65},{65,129},{129,193},{193,1... | collective-permute-start | bytes 688136 | tf_op jit(solution)/shard_map/ppermute | solution.py:22
  19.1 3.2 %collective-permute-start.16 = (bf16[128,896]{1,0:T(8,128)(2,1)S(1)}, bf16[128,896]{1,0:T(8,128)(2,1)S(1)}, u32[]{:S(2)}, u32[]{:S(2)}) collective-permute-start(bf16[128,896]{1,0:T(8,128)(2,1)S(1)} %collective-permute-done.15.rest_12_), channel_id=1, source_target_pairs={{0,192},{64,0},{128,64},{192,128},{1,193},{65,1},{129,65},{193,129... | collective-permute-start | bytes 688136 | tf_op jit(solution)/shard_map/ppermute | solution.py:22
  22.3 3.3 %select_amplitudes.3.t = bf16[8,1536,256]{2,1,0:T(8,128)(2,1)S(1)} custom-call(s32[8]{0:T(128)S(1)} %copy-done.1, s32[16]{0:T(128)S(1)} %copy-done.3, s32[1,512]{1,0:T(1,128)S(1)} %get-tuple-element.85.labels, s32[1,512]{1,0:T(1,128)S(1)} %get-tuple-element.86.rank, bf16[512,2048]{1,0:T(8,128)(2,1)S(1)} %copy-done.4, bf16[128,2048]{1,0:T(8,128)(2,1)S(1)} %join.1.rest_0_), custom_call_target="tpu_custom_call" | custom-call | flops 13200000000 | tf_op jit(solution)/shard_map/select_amplitudes/pallas_call | solution.py:228
  25.6 1.1 %collective-permute-done.13.rest_6_ = bf16[128,896]{1,0:T(8,128)(2,1)S(1)} collective-permute-done((bf16[128,896]{1,0:T(8,128)(2,1)S(1)}, bf16[128,896]{1,0:T(8,128)(2,1)S(1)}, u32[]{:S(2)}, u32[]{:S(2)}) %collective-permute-start.13) | collective-permute-done | bytes 229408 | tf_op jit(solution)/shard_map/ppermute | solution.py:22
  26.8 2.5 %collective-permute-done.14.rest_7_ = bf16[128,896]{1,0:T(8,128)(2,1)S(1)} collective-permute-done((bf16[128,896]{1,0:T(8,128)(2,1)S(1)}, bf16[128,896]{1,0:T(8,128)(2,1)S(1)}, u32[]{:S(2)}, u32[]{:S(2)}) %collective-permute-start.14) | collective-permute-done | bytes 229408 | tf_op jit(solution)/shard_map/ppermute | solution.py:22
  29.3 1.7 %product.3 = (f32[8,2,32,256]{3,2,1,0:T(8,128)S(1)}, f32[8,2,32,256]{3,2,1,0:T(8,128)S(1)}, f32[8,128]{1,0:T(8,128)S(1)}) custom-call(s32[3]{0:T(128)S(1)} %pad_add_fusion.where, s32[8]{0:T(128)S(1)} %copy-done.1, bf16[8,1536,256]{2,1,0:T(8,128)(2,1)S(1)} %select_amplitudes.3.t, bf16[128,896]{1,0:T(8,128)(2,1)S(1)} %get-tuple-element.89.rest_0_, ...), custom_call_target="tpu_custom_call" | custom-call | flops 1760000000 | tf_op jit(solution)/shard_map/product/pallas_call | solution.py:279
  31.3 0.5 collective-permute-start.19
  31.8 1.4 %collective-permute-done.19.b = f32[8,128]{1,0:T(8,128)S(1)} collective-permute-done((f32[8,128]{1,0:T(8,128)S(1)}, f32[8,128]{1,0:T(8,128)S(1)}, u32[]{:S(2)}, u32[]{:S(2)}) %collective-permute-start.19) | collective-permute-done | bytes 4128 | tf_op jit(solution)/shard_map/ppermute | solution.py:22
  33.4 24.3 %all_to_all.24 = f16[16,32,256]{2,1,0:T(8,128)(2,1)S(1)} all-to-all(f16[16,32,256]{2,1,0:T(8,128)(2,1)S(1)} %convert_element_type.32), channel_id=1, replica_groups=mesh['x'=4,'yl'=2,'vir'=8,'yh'=2,'core'=2] {'vir','yh'}, dimensions={0} | all-to-all | bytes 524288 | tf_op jit(solution)/shard_map/all_to_all | solution.py:495
  57.7 1.7 %spread.1 = (f32[32,512]{1,0:T(8,128)S(1)}, f32[8,32,128]{2,1,0:T(8,128)}) custom-call(s32[3]{0:T(128)S(1)} %pad_add_fusion.where, s32[8]{0:T(128)S(1)} %copy-done.1, s32[1,512]{1,0:T(1,128)S(1)} %get-tuple-element.85.labels, s32[1,512]{1,0:T(1,128)S(1)} %get-tuple-element.86.rank, s32[1,1024]{1,0:T(1,128)S(1)} %get-tuple-element.87.spots, ...), custom_call_target="tpu_custom_call" | custom-call | flops 1870000000 | tf_op jit(solution)/shard_map/spread/pallas_call | solution.py:352
  59.4 5.2 %all-to-all-start.4 = ((f32[8,32,128]{2,1,0:T(8,128)}), f32[8,32,128]{2,1,0:T(8,128)S(1)}, u32[]{:S(2)}, u32[]{:S(2)}) async-start(f32[8,32,128]{2,1,0:T(8,128)} %get-tuple-element.98), calls=%async_computation.4 | async-start | bytes 262144 | tf_op jit(solution)/shard_map/all_to_all | solution.py:497
  65.3 4.8 %all-to-all-done.4 = f32[8,32,128]{2,1,0:T(8,128)S(1)} async-done(((f32[8,32,128]{2,1,0:T(8,128)}), f32[8,32,128]{2,1,0:T(8,128)S(1)}, u32[]{:S(2)}, u32[]{:S(2)}) %all-to-all-start.4) | async-done | bytes 131104 | tf_op jit(solution)/shard_map/all_to_all | solution.py:497
  70.1 0.4 conditional.3
  70.5 0.6 copy-done.6
  (32 shorter events, 1.2 us)
Async XLA Ops:
  0.0 12.2 %copy-start.1 = (s32[8]{0:T(128)S(1)}, s32[8]{0:T(128)}, u32[]{:S(2)}) copy-start(s32[8]{0:T(128)} %ab.9) | copy-start | bytes 100
  0.0 12.2 %copy-start.2 = (s32[64]{0:T(128)S(1)}, s32[64]{0:T(128)}, u32[]{:S(2)}) copy-start(s32[64]{0:T(128)} %occ.1) | copy-start | bytes 772
  2.0 7.4 %collective-permute-start.7 = (bf16[128,896]{1,0:T(8,128)(2,1)S(1)}, bf16[128,896]{1,0:T(8,128)(2,1)S(1)}, u32[]{:S(2)}, u32[]{:S(2)}) collective-permute-start(bf16[128,896]{1,0:T(8,128)(2,1)S(1)} %get-tuple-element.89.rest_0_), channel_id=1, source_target_pairs={{0,32},{32,0},{1,33},{33,1},{2,34},{34,2},{3,35},{35,3},{4,36},{36... | collective-permute-start | bytes 688136 | tf_op jit(solution)/shard_map/ppermute | solution.py:22
  4.3 11.7 %collective-permute-start.8 = (bf16[128,512]{1,0:T(8,128)(2,1)S(1)}, bf16[128,512]{1,0:T(8,128)(2,1)S(1)}, u32[]{:S(2)}, u32[]{:S(2)}) collective-permute-start(bf16[128,512]{1,0:T(8,128)(2,1)S(1)} %get-tuple-element.90.refs_1_.rest_1_), channel_id=1, source_target_pairs={{0,64},{64,128},{128,192},{192,0},{1,65},{65,129},{129,193},{193,1... | collective-permute-start | bytes 393224 | tf_op jit(solution)/shard_map/ppermute | solution.py:22
  4.3 12.6 %collective-permute-start.9 = (bf16[128,512]{1,0:T(8,128)(2,1)S(1)}, bf16[128,512]{1,0:T(8,128)(2,1)S(1)}, u32[]{:S(2)}, u32[]{:S(2)}) collective-permute-start(bf16[128,512]{1,0:T(8,128)(2,1)S(1)} %get-tuple-element.90.refs_1_.rest_1_), channel_id=1, source_target_pairs={{0,128},{64,192},{128,0},{192,64},{1,129},{65,193},{129,1},{193,65... | collective-permute-start | bytes 393224 | tf_op jit(solution)/shard_map/ppermute | solution.py:22
  6.8 10.1 %collective-permute-start.10 = (bf16[128,512]{1,0:T(8,128)(2,1)S(1)}, bf16[128,512]{1,0:T(8,128)(2,1)S(1)}, u32[]{:S(2)}, u32[]{:S(2)}) collective-permute-start(bf16[128,512]{1,0:T(8,128)(2,1)S(1)} %get-tuple-element.90.refs_1_.rest_1_), channel_id=1, source_target_pairs={{0,192},{64,0},{128,64},{192,128},{1,193},{65,1},{129,65},{193,129... | collective-permute-start | bytes 393224 | tf_op jit(solution)/shard_map/ppermute | solution.py:22
  8.2 10.8 %collective-permute-start.12 = (bf16[128,896]{1,0:T(8,128)(2,1)S(1)}, bf16[128,896]{1,0:T(8,128)(2,1)S(1)}, u32[]{:S(2)}, u32[]{:S(2)}) collective-permute-start(bf16[128,896]{1,0:T(8,128)(2,1)S(1)} %get-tuple-element.89.rest_0_), channel_id=1, source_target_pairs={{0,64},{64,128},{128,192},{192,0},{1,65},{65,129},{129,193},{193,1... | collective-permute-start | bytes 688136 | tf_op jit(solution)/shard_map/ppermute | solution.py:22
  9.4 9.6 %collective-permute-start.15 = (bf16[128,896]{1,0:T(8,128)(2,1)S(1)}, bf16[128,896]{1,0:T(8,128)(2,1)S(1)}, u32[]{:S(2)}, u32[]{:S(2)}) collective-permute-start(bf16[128,896]{1,0:T(8,128)(2,1)S(1)} %collective-permute-done.7.refs_0_.rest_2_), channel_id=1, source_target_pairs={{0,192},{64,0},{128,64},{192,128},{1,193},{65,1},{129,65},{193,129... | collective-permute-start | bytes 688136 | tf_op jit(solution)/shard_map/ppermute | solution.py:22
  12.2 10.1 %copy-start.3 = (s32[16]{0:T(128)S(1)}, s32[16]{0:T(128)}, u32[]{:S(2)}) copy-start(s32[16]{0:T(128)} %cd.3) | copy-start | bytes 196
  12.2 10.1 %copy-start.4 = (bf16[512,2048]{1,0:T(8,128)(2,1)S(1)}, bf16[512,2048]{1,0:T(8,128)(2,1)}, u32[]{:S(2)}) copy-start(bf16[512,2048]{1,0:T(8,128)(2,1)} %t.1) | copy-start | bytes 6291460
  16.0 9.6 %collective-permute-start.17 = (bf16[128,896]{1,0:T(8,128)(2,1)S(1)}, bf16[128,896]{1,0:T(8,128)(2,1)S(1)}, u32[]{:S(2)}, u32[]{:S(2)}) collective-permute-start(bf16[128,896]{1,0:T(8,128)(2,1)S(1)} %get-tuple-element.89.rest_0_), channel_id=1, source_target_pairs={{0,192},{64,0},{128,64},{192,128},{1,193},{65,1},{129,65},{193,129... | collective-permute-start | bytes 688136 | tf_op jit(solution)/shard_map/ppermute | solution.py:22
  17.0 12.3 %collective-permute-start.11 = (bf16[128,2048]{1,0:T(8,128)(2,1)S(1)}, bf16[128,2048]{1,0:T(8,128)(2,1)S(1)}, u32[]{:S(2)}, u32[]{:S(2)}) collective-permute-start(bf16[128,2048]{1,0:T(8,128)(2,1)S(1)} %join.1.rest_0_), channel_id=1, source_target_pairs={{0,32},{32,0},{1,33},{33,1},{2,34},{34,2},{3,35},{35,3},{4,36},{36... | collective-permute-start | bytes 1572872 | tf_op jit(solution)/shard_map/ppermute | solution.py:22
  17.5 9.3 %collective-permute-start.13 = (bf16[128,896]{1,0:T(8,128)(2,1)S(1)}, bf16[128,896]{1,0:T(8,128)(2,1)S(1)}, u32[]{:S(2)}, u32[]{:S(2)}) collective-permute-start(bf16[128,896]{1,0:T(8,128)(2,1)S(1)} %collective-permute-done.7.refs_0_.rest_2_), channel_id=1, source_target_pairs={{0,64},{64,128},{128,192},{192,0},{1,65},{65,129},{129,193},{193,1... | collective-permute-start | bytes 688136 | tf_op jit(solution)/shard_map/ppermute | solution.py:22
  19.1 10.2 %collective-permute-start.14 = (bf16[128,896]{1,0:T(8,128)(2,1)S(1)}, bf16[128,896]{1,0:T(8,128)(2,1)S(1)}, u32[]{:S(2)}, u32[]{:S(2)}) collective-permute-start(bf16[128,896]{1,0:T(8,128)(2,1)S(1)} %collective-permute-done.12.rest_4_), channel_id=1, source_target_pairs={{0,64},{64,128},{128,192},{192,0},{1,65},{65,129},{129,193},{193,1... | collective-permute-start | bytes 688136 | tf_op jit(solution)/shard_map/ppermute | solution.py:22
  19.1 10.1 %collective-permute-start.16 = (bf16[128,896]{1,0:T(8,128)(2,1)S(1)}, bf16[128,896]{1,0:T(8,128)(2,1)S(1)}, u32[]{:S(2)}, u32[]{:S(2)}) collective-permute-start(bf16[128,896]{1,0:T(8,128)(2,1)S(1)} %collective-permute-done.15.rest_12_), channel_id=1, source_target_pairs={{0,192},{64,0},{128,64},{192,128},{1,193},{65,1},{129,65},{193,129... | collective-permute-start | bytes 688136 | tf_op jit(solution)/shard_map/ppermute | solution.py:22
  25.6 5.4 %copy-start = (bf16[128,2048]{1,0:T(8,128)(2,1)S(1)}, bf16[128,2048]{1,0:T(8,128)(2,1)}, u32[]{:S(2)}) copy-start(bf16[128,2048]{1,0:T(8,128)(2,1)} %v.1) | copy-start | bytes 1572868
  31.2 2.0 %collective-permute-start.18 = (f32[8,2,32,256]{3,2,1,0:T(8,128)S(1)}, f32[8,2,32,256]{3,2,1,0:T(8,128)S(1)}, u32[]{:S(2)}, u32[]{:S(2)}) collective-permute-start(f32[8,2,32,256]{3,2,1,0:T(8,128)S(1)} %get-tuple-element.95), channel_id=1, source_target_pairs={{0,1},{1,0},{2,3},{3,2},{4,5},{5,4},{6,7},{7,6},{8,9},{9,8},{10,11... | collective-permute-start | bytes 1572872 | tf_op jit(solution)/shard_map/ppermute | solution.py:22
  31.3 1.9 %collective-permute-start.19 = (f32[8,128]{1,0:T(8,128)S(1)}, f32[8,128]{1,0:T(8,128)S(1)}, u32[]{:S(2)}, u32[]{:S(2)}) collective-permute-start(f32[8,128]{1,0:T(8,128)S(1)} %get-tuple-element.96.a), channel_id=1, source_target_pairs={{0,1},{1,0},{2,3},{3,2},{4,5},{5,4},{6,7},{7,6},{8,9},{9,8},{10,11... | collective-permute-start | bytes 12296 | tf_op jit(solution)/shard_map/ppermute | solution.py:22
  33.4 36.7 %copy-start.5 = (bf16[512,2048]{1,0:T(8,128)(2,1)S(1)}, bf16[512,2048]{1,0:T(8,128)(2,1)}, u32[]{:S(2)}) copy-start(bf16[512,2048]{1,0:T(8,128)(2,1)} %t.1) | copy-start | bytes 6291460
  59.4 10.6 %all-to-all-start.4 = ((f32[8,32,128]{2,1,0:T(8,128)}), f32[8,32,128]{2,1,0:T(8,128)S(1)}, u32[]{:S(2)}, u32[]{:S(2)}) async-start(f32[8,32,128]{2,1,0:T(8,128)} %get-tuple-element.98), calls=%async_computation.4 | async-start | bytes 262144 | tf_op jit(solution)/shard_map/all_to_all | solution.py:497
  70.5 0.6 copy-start.6

commit v6 on v5

--- a/solution.py
+++ b/solution.py
@@ -264,7 +264,11 @@
             for out, c in ((keep, core), (send, 1 - core)):
                 row = pl.multiple_of((2 * half + c) * part, part)
                 out[v, half] = acc[pl.ds(row, part), :]
-    largest[...] = jnp.full(largest.shape, jnp.max(most), jnp.float32)
+    top = jnp.full(largest.shape, jnp.max(most), jnp.float32)
+    largest[...] = top
+    lane = lax.broadcasted_iota(jnp.int32, top.shape, 1)
+    spare = send[send.shape[0] - 1, 1, 0:8, ROWS - TILE :]
+    send[send.shape[0] - 1, 1, 0:8, ROWS - TILE :] = jnp.where(lane < TILE - SCALES, spare, top)
 
 
 def product(where, ab, t, blocks):
@@ -288,8 +292,8 @@
     )(where, ab, t, *arrays)
 
 
-def combine_kernel(keep, got, a, b, out):
-    top = (a[...] + b[...])[0:1, :]
+def combine_kernel(keep, got, a, out):
+    top = a[0:1, :] + got[got.shape[0] - 1, 1, 0:1, ROWS - TILE :][:, TILE - 1 :]
     up, down = jnp.ones_like(top), jnp.ones_like(top)
     for bits in (64, 32, 8, 4, 2, 1):
         fits = top * (up * 2.0**bits) <= 2.0**15
@@ -307,16 +311,16 @@
             out[v * keep.shape[1] + y] = (keep[v, y] + got[v, y]) * up + parts
 
 
-def combine(keep, got, a, b):
+def combine(keep, got, a):
     return pl.pallas_call(
         combine_kernel,
         out_shape=jax.ShapeDtypeStruct((keep.shape[0] * keep.shape[1],) + keep.shape[2:], jnp.float32),
-        in_specs=[VMEM] * 4,
+        in_specs=[VMEM] * 3,
         out_specs=VMEM,
         compiler_params=params(6),
         cost_estimate=cost(1.2),
         name="combine",
-    )(keep, got, a, b)
+    )(keep, got, a)
 
 
 def spread_kernel(where, ab, labels, rank, spots, parts, own, send):
@@ -491,7 +495,7 @@
     )
     labels, rank, spots, over = found
     other = shifted("core", 2, 1)
-    part = combine(keep, other(send), largest, other(largest)).astype(jnp.float16)
+    part = combine(keep, other(send), largest).astype(jnp.float16)
     part = lax.all_to_all(part, ("vir", "yh"), 0, 0, tiled=True).astype(jnp.float32)
     own, send = spread(where, ab_irrep, labels, rank, spots, part)
     got = lax.all_to_all(send, ("x", "yl"), 0, 0, tiled=True)

time: 71.4 us -> 71.3 us (level)
    ppermute x13 -> x12, starting transfers between devices: 16.4 us -> 15.9 us  [shifted(): lax.ppermute(a, axis, [(i, (i + step) % size) for i in range(size)])]
    ppermute x13 -> x12, waiting for transfers between devices: 5.69 us -> 6.17 us  [shifted(): lax.ppermute(a, axis, [(i, (i + step) % size) for i in range(size)])]
  transfers between devices with their start and end apart: 14 -> 13, of which waited for: 5 -> 5; matrix products, arithmetic and copies ran while one was open for 0% -> 0% of each run, Pallas kernels for 9% -> 9%
where the time goes in v6:
time: 71.3 us; the launch traced here: 71 us
  blocking collectives  24.3 us (34%)
  starting transfers between devices  21 us (29%)
  Pallas kernels  12.3 us (17%)
  waiting for transfers between devices  11 us (15%)
  between operations  1.36 us (2%)
    all_to_all x1, blocking collectives, per_device(): lax.all_to_all(part, ('vir', 'yh'), 0, 0, tiled=True).astype(jnp.float32)  24.3 us
    ppermute x12, starting transfers between devices, shifted(): lax.ppermute(a, axis, [(i, (i + step) % size) for i in range(size)])  15.9 us
    ppermute x12, waiting for transfers between devices, shifted(): lax.ppermute(a, axis, [(i, (i + step) % size) for i in range(size)])  6.17 us
    all_to_all x1, starting transfers between devices, per_device(): got = lax.all_to_all(send, ('x', 'yl'), 0, 0, tiled=True)  5.15 us
    all_to_all x1, waiting for transfers between devices, per_device(): got = lax.all_to_all(send, ('x', 'yl'), 0, 0, tiled=True)  4.79 us
    pallas_call x1, Pallas kernels, select(): pl.pallas_call(functools.partial(select_kernel, skip, len(after)), out_sh...  3.28 us
    pallas_call x1, Pallas kernels, ranks(): pl.pallas_call(functools.partial(rank_kernel, len(after)), out_shape=[jax...  3.09 us
    pallas_call x1, Pallas kernels, pack(): pl.pallas_call(functools.partial(pack_kernel, skip), out_shape=[jax.Shape...  1.93 us
  transfers between devices with their start and end apart: 13, of which 5 were waited for; matrix products, arithmetic and copies ran while one was open for 0% of the time, Pallas kernels for 9%

profile of v6, /device:TPU:8, one launch (start us, length us, event | category | flops | bytes accessed | tf_op | source)
XLA Modules:
  0.0 71.0 jit_solution(6044841780602917854)
XLA Ops:
  0.1 1.9 %pack_integrals.3 = (s32[1]{0:T(128)}, bf16[128,896]{1,0:T(8,128)(2,1)S(1)}, bf16[128,512]{1,0:T(8,128)(2,1)S(1)}) custom-call(s32[3]{0:T(128)S(1)} %pad_add_fusion.where, s32[8]{0:T(128)} %ab.9, s32[16]{0:T(128)} %cd.3, bf16[128,2048]{1,0:T(8,128)(2,1)} %v.1), custom_call_target="tpu_custom_call" | custom-call | flops 2200000000 | tf_op jit(solution)/shard_map/pack_integrals/pallas_call | solution.py:75
  2.0 2.3 %collective-permute-start.7 = (bf16[128,896]{1,0:T(8,128)(2,1)S(1)}, bf16[128,896]{1,0:T(8,128)(2,1)S(1)}, u32[]{:S(2)}, u32[]{:S(2)}) collective-permute-start(bf16[128,896]{1,0:T(8,128)(2,1)S(1)} %get-tuple-element.89.rest_0_), channel_id=1, source_target_pairs={{0,32},{32,0},{1,33},{33,1},{2,34},{34,2},{3,35},{35,3},{4,36},{36... | collective-permute-start | bytes 688136 | tf_op jit(solution)/shard_map/ppermute | solution.py:22
  4.3 2.5 %collective-permute-start.9 = (bf16[128,512]{1,0:T(8,128)(2,1)S(1)}, bf16[128,512]{1,0:T(8,128)(2,1)S(1)}, u32[]{:S(2)}, u32[]{:S(2)}) collective-permute-start(bf16[128,512]{1,0:T(8,128)(2,1)S(1)} %get-tuple-element.90.refs_1_.rest_1_), channel_id=1, source_target_pairs={{0,128},{64,192},{128,0},{192,64},{1,129},{65,193},{129,1},{193,65... | collective-permute-start | bytes 393224 | tf_op jit(solution)/shard_map/ppermute | solution.py:22
  6.8 1.4 %collective-permute-start.10 = (bf16[128,512]{1,0:T(8,128)(2,1)S(1)}, bf16[128,512]{1,0:T(8,128)(2,1)S(1)}, u32[]{:S(2)}, u32[]{:S(2)}) collective-permute-start(bf16[128,512]{1,0:T(8,128)(2,1)S(1)} %get-tuple-element.90.refs_1_.rest_1_), channel_id=1, source_target_pairs={{0,192},{64,0},{128,64},{192,128},{1,193},{65,1},{129,65},{193,129... | collective-permute-start | bytes 393224 | tf_op jit(solution)/shard_map/ppermute | solution.py:22
  8.2 0.6 collective-permute-start.12
  8.8 0.6 collective-permute-done.7.refs_0_.rest_2_
  9.4 2.8 %collective-permute-start.15 = (bf16[128,896]{1,0:T(8,128)(2,1)S(1)}, bf16[128,896]{1,0:T(8,128)(2,1)S(1)}, u32[]{:S(2)}, u32[]{:S(2)}) collective-permute-start(bf16[128,896]{1,0:T(8,128)(2,1)S(1)} %collective-permute-done.7.refs_0_.rest_2_), channel_id=1, source_target_pairs={{0,192},{64,0},{128,64},{192,128},{1,193},{65,1},{129,65},{193,129... | collective-permute-start | bytes 688136 | tf_op jit(solution)/shard_map/ppermute | solution.py:22
  12.2 3.1 %ranks.1 = (s32[1,512]{1,0:T(1,128)S(1)}, s32[1,512]{1,0:T(1,128)S(1)}, s32[1,1024]{1,0:T(1,128)S(1)}, s32[1]{0:T(128)}) custom-call(s32[3]{0:T(128)S(1)} %pad_add_fusion.where, s32[64]{0:T(128)S(1)} %copy-done.2, s32[8]{0:T(128)S(1)} %copy-done.1, s32[1,64]{1,0:T(1,128)S(1)} %bitcast.43), custom_call_target="tpu_custom_call" | custom-call | flops 3630000128 | tf_op jit(solution)/shard_map/ranks/pallas_call | solution.py:163
  15.9 0.9 %collective-permute-start.17 = (bf16[128,896]{1,0:T(8,128)(2,1)S(1)}, bf16[128,896]{1,0:T(8,128)(2,1)S(1)}, u32[]{:S(2)}, u32[]{:S(2)}) collective-permute-start(bf16[128,896]{1,0:T(8,128)(2,1)S(1)} %get-tuple-element.89.rest_0_), channel_id=1, source_target_pairs={{0,192},{64,0},{128,64},{192,128},{1,193},{65,1},{129,65},{193,129... | collective-permute-start | bytes 688136 | tf_op jit(solution)/shard_map/ppermute | solution.py:22
  16.8 0.6 collective-permute-start.11
  17.4 1.6 %collective-permute-start.13 = (bf16[128,896]{1,0:T(8,128)(2,1)S(1)}, bf16[128,896]{1,0:T(8,128)(2,1)S(1)}, u32[]{:S(2)}, u32[]{:S(2)}) collective-permute-start(bf16[128,896]{1,0:T(8,128)(2,1)S(1)} %collective-permute-done.7.refs_0_.rest_2_), channel_id=1, source_target_pairs={{0,64},{64,128},{128,192},{192,0},{1,65},{65,129},{129,193},{193,1... | collective-permute-start | bytes 688136 | tf_op jit(solution)/shard_map/ppermute | solution.py:22
  19.0 3.2 %collective-permute-start.16 = (bf16[128,896]{1,0:T(8,128)(2,1)S(1)}, bf16[128,896]{1,0:T(8,128)(2,1)S(1)}, u32[]{:S(2)}, u32[]{:S(2)}) collective-permute-start(bf16[128,896]{1,0:T(8,128)(2,1)S(1)} %collective-permute-done.15.rest_12_), channel_id=1, source_target_pairs={{0,192},{64,0},{128,64},{192,128},{1,193},{65,1},{129,65},{193,129... | collective-permute-start | bytes 688136 | tf_op jit(solution)/shard_map/ppermute | solution.py:22
  22.2 3.3 %select_amplitudes.3.t = bf16[8,1536,256]{2,1,0:T(8,128)(2,1)S(1)} custom-call(s32[8]{0:T(128)S(1)} %copy-done.1, s32[16]{0:T(128)S(1)} %copy-done.3, s32[1,512]{1,0:T(1,128)S(1)} %get-tuple-element.85.labels, s32[1,512]{1,0:T(1,128)S(1)} %get-tuple-element.86.rank, bf16[512,2048]{1,0:T(8,128)(2,1)S(1)} %copy-done.4, bf16[128,2048]{1,0:T(8,128)(2,1)S(1)} %join.1.rest_0_), custom_call_target="tpu_custom_call" | custom-call | flops 13200000000 | tf_op jit(solution)/shard_map/select_amplitudes/pallas_call | solution.py:228
  25.5 1.2 %collective-permute-done.13.rest_6_ = bf16[128,896]{1,0:T(8,128)(2,1)S(1)} collective-permute-done((bf16[128,896]{1,0:T(8,128)(2,1)S(1)}, bf16[128,896]{1,0:T(8,128)(2,1)S(1)}, u32[]{:S(2)}, u32[]{:S(2)}) %collective-permute-start.13) | collective-permute-done | bytes 229408 | tf_op jit(solution)/shard_map/ppermute | solution.py:22
  26.7 2.5 %collective-permute-done.14.rest_7_ = bf16[128,896]{1,0:T(8,128)(2,1)S(1)} collective-permute-done((bf16[128,896]{1,0:T(8,128)(2,1)S(1)}, bf16[128,896]{1,0:T(8,128)(2,1)S(1)}, u32[]{:S(2)}, u32[]{:S(2)}) %collective-permute-start.14) | collective-permute-done | bytes 229408 | tf_op jit(solution)/shard_map/ppermute | solution.py:22
  29.1 1.7 %product.3 = (f32[8,2,32,256]{3,2,1,0:T(8,128)S(1)}, f32[8,2,32,256]{3,2,1,0:T(8,128)S(1)}, f32[8,128]{1,0:T(8,128)S(1)}) custom-call(s32[3]{0:T(128)S(1)} %pad_add_fusion.where, s32[8]{0:T(128)S(1)} %copy-done.1, bf16[8,1536,256]{2,1,0:T(8,128)(2,1)S(1)} %select_amplitudes.3.t, bf16[128,896]{1,0:T(8,128)(2,1)S(1)} %get-tuple-element.89.rest_0_, ...), custom_call_target="tpu_custom_call" | custom-call | flops 1760000000 | tf_op jit(solution)/shard_map/product/pallas_call | solution.py:283
  31.2 1.9 %collective-permute-done.18.got = f32[8,2,32,256]{3,2,1,0:T(8,128)S(1)} collective-permute-done((f32[8,2,32,256]{3,2,1,0:T(8,128)S(1)}, f32[8,2,32,256]{3,2,1,0:T(8,128)S(1)}, u32[]{:S(2)}, u32[]{:S(2)}) %collective-permute-start.18) | collective-permute-done | bytes 524320 | tf_op jit(solution)/shard_map/ppermute | solution.py:22
  33.3 24.3 %all_to_all.24 = f16[16,32,256]{2,1,0:T(8,128)(2,1)S(1)} all-to-all(f16[16,32,256]{2,1,0:T(8,128)(2,1)S(1)} %convert_element_type.32), channel_id=1, replica_groups=mesh['x'=4,'yl'=2,'vir'=8,'yh'=2,'core'=2] {'vir','yh'}, dimensions={0} | all-to-all | bytes 524288 | tf_op jit(solution)/shard_map/all_to_all | solution.py:499
  57.7 1.7 %spread.1 = (f32[32,512]{1,0:T(8,128)S(1)}, f32[8,32,128]{2,1,0:T(8,128)}) custom-call(s32[3]{0:T(128)S(1)} %pad_add_fusion.where, s32[8]{0:T(128)S(1)} %copy-done.1, s32[1,512]{1,0:T(1,128)S(1)} %get-tuple-element.85.labels, s32[1,512]{1,0:T(1,128)S(1)} %get-tuple-element.86.rank, s32[1,1024]{1,0:T(1,128)S(1)} %get-tuple-element.87.spots, ...), custom_call_target="tpu_custom_call" | custom-call | flops 1870000000 | tf_op jit(solution)/shard_map/spread/pallas_call | solution.py:356
  59.4 5.2 %all-to-all-start.4 = ((f32[8,32,128]{2,1,0:T(8,128)}), f32[8,32,128]{2,1,0:T(8,128)S(1)}, u32[]{:S(2)}, u32[]{:S(2)}) async-start(f32[8,32,128]{2,1,0:T(8,128)} %get-tuple-element.98), calls=%async_computation.4 | async-start | bytes 262144 | tf_op jit(solution)/shard_map/all_to_all | solution.py:501
  65.2 4.8 %all-to-all-done.4 = f32[8,32,128]{2,1,0:T(8,128)S(1)} async-done(((f32[8,32,128]{2,1,0:T(8,128)}), f32[8,32,128]{2,1,0:T(8,128)S(1)}, u32[]{:S(2)}, u32[]{:S(2)}) %all-to-all-start.4) | async-done | bytes 131104 | tf_op jit(solution)/shard_map/all_to_all | solution.py:501
  70.0 0.4 conditional.3
  70.0 0.4 finish.1
  70.4 0.6 copy-done.6
  (30 shorter events, 0.8 us)
Async XLA Ops:
  0.0 12.2 %copy-start.1 = (s32[8]{0:T(128)S(1)}, s32[8]{0:T(128)}, u32[]{:S(2)}) copy-start(s32[8]{0:T(128)} %ab.9) | copy-start | bytes 100
  0.0 12.2 %copy-start.2 = (s32[64]{0:T(128)S(1)}, s32[64]{0:T(128)}, u32[]{:S(2)}) copy-start(s32[64]{0:T(128)} %occ.1) | copy-start | bytes 772
  2.0 7.4 %collective-permute-start.7 = (bf16[128,896]{1,0:T(8,128)(2,1)S(1)}, bf16[128,896]{1,0:T(8,128)(2,1)S(1)}, u32[]{:S(2)}, u32[]{:S(2)}) collective-permute-start(bf16[128,896]{1,0:T(8,128)(2,1)S(1)} %get-tuple-element.89.rest_0_), channel_id=1, source_target_pairs={{0,32},{32,0},{1,33},{33,1},{2,34},{34,2},{3,35},{35,3},{4,36},{36... | collective-permute-start | bytes 688136 | tf_op jit(solution)/shard_map/ppermute | solution.py:22
  4.3 11.6 %collective-permute-start.8 = (bf16[128,512]{1,0:T(8,128)(2,1)S(1)}, bf16[128,512]{1,0:T(8,128)(2,1)S(1)}, u32[]{:S(2)}, u32[]{:S(2)}) collective-permute-start(bf16[128,512]{1,0:T(8,128)(2,1)S(1)} %get-tuple-element.90.refs_1_.rest_1_), channel_id=1, source_target_pairs={{0,64},{64,128},{128,192},{192,0},{1,65},{65,129},{129,193},{193,1... | collective-permute-start | bytes 393224 | tf_op jit(solution)/shard_map/ppermute | solution.py:22
  4.3 12.5 %collective-permute-start.9 = (bf16[128,512]{1,0:T(8,128)(2,1)S(1)}, bf16[128,512]{1,0:T(8,128)(2,1)S(1)}, u32[]{:S(2)}, u32[]{:S(2)}) collective-permute-start(bf16[128,512]{1,0:T(8,128)(2,1)S(1)} %get-tuple-element.90.refs_1_.rest_1_), channel_id=1, source_target_pairs={{0,128},{64,192},{128,0},{192,64},{1,129},{65,193},{129,1},{193,65... | collective-permute-start | bytes 393224 | tf_op jit(solution)/shard_map/ppermute | solution.py:22
  6.8 10.0 %collective-permute-start.10 = (bf16[128,512]{1,0:T(8,128)(2,1)S(1)}, bf16[128,512]{1,0:T(8,128)(2,1)S(1)}, u32[]{:S(2)}, u32[]{:S(2)}) collective-permute-start(bf16[128,512]{1,0:T(8,128)(2,1)S(1)} %get-tuple-element.90.refs_1_.rest_1_), channel_id=1, source_target_pairs={{0,192},{64,0},{128,64},{192,128},{1,193},{65,1},{129,65},{193,129... | collective-permute-start | bytes 393224 | tf_op jit(solution)/shard_map/ppermute | solution.py:22
  8.2 10.7 %collective-permute-start.12 = (bf16[128,896]{1,0:T(8,128)(2,1)S(1)}, bf16[128,896]{1,0:T(8,128)(2,1)S(1)}, u32[]{:S(2)}, u32[]{:S(2)}) collective-permute-start(bf16[128,896]{1,0:T(8,128)(2,1)S(1)} %get-tuple-element.89.rest_0_), channel_id=1, source_target_pairs={{0,64},{64,128},{128,192},{192,0},{1,65},{65,129},{129,193},{193,1... | collective-permute-start | bytes 688136 | tf_op jit(solution)/shard_map/ppermute | solution.py:22
  9.4 9.5 %collective-permute-start.15 = (bf16[128,896]{1,0:T(8,128)(2,1)S(1)}, bf16[128,896]{1,0:T(8,128)(2,1)S(1)}, u32[]{:S(2)}, u32[]{:S(2)}) collective-permute-start(bf16[128,896]{1,0:T(8,128)(2,1)S(1)} %collective-permute-done.7.refs_0_.rest_2_), channel_id=1, source_target_pairs={{0,192},{64,0},{128,64},{192,128},{1,193},{65,1},{129,65},{193,129... | collective-permute-start | bytes 688136 | tf_op jit(solution)/shard_map/ppermute | solution.py:22
  12.2 10.0 %copy-start.3 = (s32[16]{0:T(128)S(1)}, s32[16]{0:T(128)}, u32[]{:S(2)}) copy-start(s32[16]{0:T(128)} %cd.3) | copy-start | bytes 196
  12.2 10.0 %copy-start.4 = (bf16[512,2048]{1,0:T(8,128)(2,1)S(1)}, bf16[512,2048]{1,0:T(8,128)(2,1)}, u32[]{:S(2)}) copy-start(bf16[512,2048]{1,0:T(8,128)(2,1)} %t.1) | copy-start | bytes 6291460
  15.9 9.6 %collective-permute-start.17 = (bf16[128,896]{1,0:T(8,128)(2,1)S(1)}, bf16[128,896]{1,0:T(8,128)(2,1)S(1)}, u32[]{:S(2)}, u32[]{:S(2)}) collective-permute-start(bf16[128,896]{1,0:T(8,128)(2,1)S(1)} %get-tuple-element.89.rest_0_), channel_id=1, source_target_pairs={{0,192},{64,0},{128,64},{192,128},{1,193},{65,1},{129,65},{193,129... | collective-permute-start | bytes 688136 | tf_op jit(solution)/shard_map/ppermute | solution.py:22
  16.8 12.3 %collective-permute-start.11 = (bf16[128,2048]{1,0:T(8,128)(2,1)S(1)}, bf16[128,2048]{1,0:T(8,128)(2,1)S(1)}, u32[]{:S(2)}, u32[]{:S(2)}) collective-permute-start(bf16[128,2048]{1,0:T(8,128)(2,1)S(1)} %join.1.rest_0_), channel_id=1, source_target_pairs={{0,32},{32,0},{1,33},{33,1},{2,34},{34,2},{3,35},{35,3},{4,36},{36... | collective-permute-start | bytes 1572872 | tf_op jit(solution)/shard_map/ppermute | solution.py:22
  17.4 9.3 %collective-permute-start.13 = (bf16[128,896]{1,0:T(8,128)(2,1)S(1)}, bf16[128,896]{1,0:T(8,128)(2,1)S(1)}, u32[]{:S(2)}, u32[]{:S(2)}) collective-permute-start(bf16[128,896]{1,0:T(8,128)(2,1)S(1)} %collective-permute-done.7.refs_0_.rest_2_), channel_id=1, source_target_pairs={{0,64},{64,128},{128,192},{192,0},{1,65},{65,129},{129,193},{193,1... | collective-permute-start | bytes 688136 | tf_op jit(solution)/shard_map/ppermute | solution.py:22
  18.9 10.2 %collective-permute-start.14 = (bf16[128,896]{1,0:T(8,128)(2,1)S(1)}, bf16[128,896]{1,0:T(8,128)(2,1)S(1)}, u32[]{:S(2)}, u32[]{:S(2)}) collective-permute-start(bf16[128,896]{1,0:T(8,128)(2,1)S(1)} %collective-permute-done.12.rest_4_), channel_id=1, source_target_pairs={{0,64},{64,128},{128,192},{192,0},{1,65},{65,129},{129,193},{193,1... | collective-permute-start | bytes 688136 | tf_op jit(solution)/shard_map/ppermute | solution.py:22
  19.0 10.1 %collective-permute-start.16 = (bf16[128,896]{1,0:T(8,128)(2,1)S(1)}, bf16[128,896]{1,0:T(8,128)(2,1)S(1)}, u32[]{:S(2)}, u32[]{:S(2)}) collective-permute-start(bf16[128,896]{1,0:T(8,128)(2,1)S(1)} %collective-permute-done.15.rest_12_), channel_id=1, source_target_pairs={{0,192},{64,0},{128,64},{192,128},{1,193},{65,1},{129,65},{193,129... | collective-permute-start | bytes 688136 | tf_op jit(solution)/shard_map/ppermute | solution.py:22
  25.5 5.4 %copy-start = (bf16[128,2048]{1,0:T(8,128)(2,1)S(1)}, bf16[128,2048]{1,0:T(8,128)(2,1)}, u32[]{:S(2)}) copy-start(bf16[128,2048]{1,0:T(8,128)(2,1)} %v.1) | copy-start | bytes 1572868
  31.1 2.0 %collective-permute-start.18 = (f32[8,2,32,256]{3,2,1,0:T(8,128)S(1)}, f32[8,2,32,256]{3,2,1,0:T(8,128)S(1)}, u32[]{:S(2)}, u32[]{:S(2)}) collective-permute-start(f32[8,2,32,256]{3,2,1,0:T(8,128)S(1)} %get-tuple-element.95), channel_id=1, source_target_pairs={{0,1},{1,0},{2,3},{3,2},{4,5},{5,4},{6,7},{7,6},{8,9},{9,8},{10,11... | collective-permute-start | bytes 1572872 | tf_op jit(solution)/shard_map/ppermute | solution.py:22
  33.3 36.7 %copy-start.5 = (bf16[512,2048]{1,0:T(8,128)(2,1)S(1)}, bf16[512,2048]{1,0:T(8,128)(2,1)}, u32[]{:S(2)}) copy-start(bf16[512,2048]{1,0:T(8,128)(2,1)} %t.1) | copy-start | bytes 6291460
  59.4 10.6 %all-to-all-start.4 = ((f32[8,32,128]{2,1,0:T(8,128)}), f32[8,32,128]{2,1,0:T(8,128)S(1)}, u32[]{:S(2)}, u32[]{:S(2)}) async-start(f32[8,32,128]{2,1,0:T(8,128)} %get-tuple-element.98), calls=%async_computation.4 | async-start | bytes 262144 | tf_op jit(solution)/shard_map/all_to_all | solution.py:501
  70.4 0.6 copy-start.6
